TPU v7x, 256 devices: a whole 4x4x8 slice. The times are simulated.
256 devices in a mesh: theta: 64 (over z, y_hi, x), rad: 4 (over y_lo, core).
Axes of the slice: x: 4, y: 4 (y_hi: 2, y_lo: 2; y = y_hi * 2 + y_lo), z: 8, core: 2. Of those that a mesh axis runs over, the one named last changes fastest.
Arguments:
- displacement: float32 [3, 768, 128, 320], P(None, 'theta', 'rad'), may hold values from -24 to 24
- stiffness: float32 [768, 128, 320], P('theta', 'rad'), may hold values from 0.1 to 10
- wall: int32 [768, 128, 320], P('theta', 'rad'), may hold values from 0 to 1, as said below
Outputs:
- moved: float32 [3, 768, 128, 320], P(None, 'theta', 'rad')
- residual_norm: float32 [], replicated
Inputs may be any that keep to these rules, and one draw needn't show every extreme that they name: wall is 1 on the first and last radial rows and on thin sheared blade surfaces that cross the radial span.
All inputs are finite; a program needn't handle non-finite values.
Results may differ from a plain program's by a relative error of at most 0.00002.
Values sent between devices are 32-bit elements; how exact they have to be, the bound alone decides.
A program may use at most 128 MiB of HBM per device.

v0:
```python
import jax
import jax.numpy as jnp
from jax import lax
from jax.sharding import PartitionSpec as P

SWEEPS = 2


RELAX_FACTOR = 1.5


def with_halo(x, sides, width):
    for axis, dim in sides:
        count, length = (lax.axis_size(axis), x.shape[dim])
        up = [(i, (i + 1) % count) for i in range(count)]
        down = [(j, i) for i, j in up]
        last = lax.slice_in_dim(x, length - width, length, axis=dim)
        initial = lax.slice_in_dim(x, 0, width, axis=dim)
        before = lax.ppermute(last, axis, up)
        after = lax.ppermute(initial, axis, down)
        x = jnp.concatenate([before, x, after], axis=dim)
    return x


def beside_all(values):
    center = values[..., 1:-1, 1:-1, 1:-1]
    neighbours = [
        values[..., 2:, 1:-1, 1:-1],
        values[..., :-2, 1:-1, 1:-1],
        values[..., 1:-1, 2:, 1:-1],
        values[..., 1:-1, :-2, 1:-1],
        values[..., 1:-1, 1:-1, 2:],
        values[..., 1:-1, 1:-1, :-2],
    ]
    return (center, neighbours)


def make_weights(coeff):
    padded = jnp.pad(coeff, ((0, 0), (0, 0), (1, 1)), mode="edge")
    center, neighbours = beside_all(padded)
    weights = [0.5 * (center + other) for other in neighbours]
    total_weight = weights[0]
    for index in range(1, 6):
        total_weight = total_weight + weights[index]
    return (weights, total_weight)


def relax(extended, weights, total_weight, chosen):
    padded = jnp.pad(extended, ((0, 0), (0, 0), (0, 0), (1, 1)))
    center, neighbours = beside_all(padded)
    weighted = weights[0] * neighbours[0]
    for index in range(1, 6):
        weighted = weighted + weights[index] * neighbours[index]
    average = weighted / total_weight
    updated = center + RELAX_FACTOR * (average - center)
    return (jnp.where(chosen, updated, center), average - center)


def shards(displacement, stiffness, wall):
    planes, radial_rows, axial_cells = stiffness.shape
    at_first = lax.axis_index("rad") == 0
    at_last = lax.axis_index("rad") == lax.axis_size("rad") - 1
    shape = (planes, radial_rows, axial_cells)
    plane_start = lax.axis_index("theta") * planes
    row_start = lax.axis_index("rad") * radial_rows
    parity = (
        lax.broadcasted_iota(jnp.int32, shape, 0)
        + plane_start
        + lax.broadcasted_iota(jnp.int32, shape, 1)
        + row_start
        + lax.broadcasted_iota(jnp.int32, shape, 2)
    ) % 2

    def low_rim(margin):
        row_index = jnp.arange(radial_rows + 2 * margin)
        return ((row_index < margin) & at_first, (row_index >= radial_rows + margin) & at_last)

    def inside(margin):
        lower, upper = low_rim(margin)
        return jnp.logical_not(lower | upper)[:, None]

    free_point = wall == 0
    red_chosen = (parity == 0) & free_point
    black_chosen = (parity == 1) & free_point
    field = displacement

    def faces(values):
        extended = with_halo(values, (("theta", 1), ("rad", 2)), 1)
        return jnp.where(inside(1), extended, 0.0)

    coeff_ext = with_halo(stiffness, (("theta", 0), ("rad", 1)), 1)
    coeff = coeff_ext
    lower, upper = low_rim(1)
    coeff = jnp.where(lower[None, :, None], coeff[:, 1 : 1 + 1, :], coeff)
    edge_row = radial_rows + 1 - 1
    weights, total_weight = make_weights(
        jnp.where(upper[None, :, None], coeff[:, edge_row : edge_row + 1, :], coeff)
    )
    for sweep in range(SWEEPS):
        field, unused = relax(faces(field), weights, total_weight, red_chosen)
        field, unused = relax(faces(field), weights, total_weight, black_chosen)
    unused_field, residual = relax(faces(field), weights, total_weight, free_point)
    residual = jnp.where(free_point, residual, 0.0)
    squared = lax.psum(jnp.sum(residual * residual), ("theta", "rad"))
    count = 3.0 * planes * radial_rows * axial_cells * lax.axis_size("theta") * lax.axis_size("rad")
    return (field, jnp.sqrt(squared / count))


def solution(mesh):
    placed = (P(None, "theta", "rad", None), P("theta", "rad", None), P("theta", "rad", None))
    return jax.shard_map(
        shards,
        mesh=mesh,
        in_specs=placed,
        out_specs=(P(None, "theta", "rad", None), P()),
        check_vma=False,
    )
```

profile of v0, /device:TPU:1, one launch (start us, length us, event | category | flops | bytes accessed | tf_op | source)
XLA Modules:
  0.0 203.1 jit_solution(12543802272681456379)
XLA Ops:
  1.5 11.3 %collective-permute-start.5 = (f32[1,32,320]{2,1,0:T(8,128)S(1)}, f32[1,32,320]{2,1,0:T(8,128)S(1)}, u32[]{:S(2)}, u32[]{:S(2)}) collective-permute-start(f32[1,32,320]{2,1,0:T(8,128)S(1)} %get-tuple-element.35), channel_id=1, source_target_pairs={{4,0},{8,4},{12,8},{16,12},{20,16},{24,20},{28,24},{32,28},{36,32}... | collective-permute-start | bytes 122888 | tf_op jit(solution)/shard_map/ppermute | solution.py:20
  12.8 1.0 fusion.72
  13.8 7.3 %collective-permute-start.1 = (f32[3,1,32,320]{3,2,1,0:T(8,128)S(1)}, f32[3,1,32,320]{3,2,1,0:T(8,128)S(1)}, u32[]{:S(2)}, u32[]{:S(2)}) collective-permute-start(f32[3,1,32,320]{3,2,1,0:T(8,128)S(1)} %get-tuple-element.29), channel_id=1, source_target_pairs={{4,0},{8,4},{12,8},{16,12},{20,16},{24,20},{28,24},{32,28},{36,32}... | collective-permute-start | bytes 368648 | tf_op jit(solution)/shard_map/ppermute | solution.py:20
  21.1 1.5 compare_and_fusion.1
  23.3 1.9 collective-permute-start.6
  25.2 0.9 collective-permute-done.6
  26.1 2.3 %collective-permute-done.7 = f32[14,1,320]{2,1,0:T(1,128)S(1)} collective-permute-done((f32[14,1,320]{2,1,0:T(1,128)S(1)}, f32[14,1,320]{2,1,0:T(1,128)S(1)}, u32[]{:S(2)}, u32[]{:S(2)}) %collective-permute-start.7) | collective-permute-done | bytes 17952 | tf_op jit(solution)/shard_map/ppermute | solution.py:20
  28.9 1.9 collective-permute-done
  31.1 3.0 %collective-permute-start.2 = (f32[3,14,1,320]{3,2,1,0:T(1,128)S(1)}, f32[3,14,1,320]{3,2,1,0:T(1,128)S(1)}, u32[]{:S(2)}, u32[]{:S(2)}) collective-permute-start(f32[3,14,1,320]{3,2,1,0:T(1,128)S(1)} %get-tuple-element.19), channel_id=1, source_target_pairs={{0,1},{1,2},{2,3},{3,0},{4,5},{5,6},{6,7},{7,4},{8,9},{9,10},{10,1... | collective-permute-start | bytes 161288 | tf_op jit(solution)/shard_map/ppermute | solution.py:19
  34.9 4.1 %collective-permute-done.2 = f32[3,14,1,320]{3,2,1,0:T(1,128)S(1)} collective-permute-done((f32[3,14,1,320]{3,2,1,0:T(1,128)S(1)}, f32[3,14,1,320]{3,2,1,0:T(1,128)S(1)}, u32[]{:S(2)}, u32[]{:S(2)}) %collective-permute-start.2) | collective-permute-done | bytes 53792 | tf_op jit(solution)/shard_map/ppermute | solution.py:19
  39.0 1.4 collective-permute-done.3
  40.9 2.6 %add_select_fusion.3 = f32[3,12,32,320]{3,2,1,0:T(8,128)S(1)} fusion(f32[3,14,34,320]{3,2,1,0:T(8,128)S(1)} %maximum_select_fusion, f32[12,32,320]{2,1,0:T(8,128)S(1)} %get-tuple-element.4, f32[12,32,320]{2,1,0:T(8,128)S(1)} %get-tuple-element.10, f32[12,32,320]{2,1,0:T(8,128)S(1)} %get-tuple-element.9, f32[12,32,320]{2,1,0:T(8,128)S(1)} %get-tuple-element.8, ...), kind=kLoop, calls=%fused_computation.3 | loop fusion | flops 5898240 | bytes 17178624 | tf_op jit(solution)/shard_map/jit(_where)/select_n | solution.py:56
  43.6 7.2 %collective-permute-start.9 = (f32[3,1,32,320]{3,2,1,0:T(8,128)S(1)}, f32[3,1,32,320]{3,2,1,0:T(8,128)S(1)}, u32[]{:S(2)}, u32[]{:S(2)}) collective-permute-start(f32[3,1,32,320]{3,2,1,0:T(8,128)S(1)} %get-tuple-element.28), channel_id=1, source_target_pairs={{4,0},{8,4},{12,8},{16,12},{20,16},{24,20},{28,24},{32,28},{36,32}... | collective-permute-start | bytes 368648 | tf_op jit(solution)/shard_map/ppermute | solution.py:20
  50.8 3.6 %collective-permute-done.8 = f32[3,1,32,320]{3,2,1,0:T(8,128)S(1)} collective-permute-done((f32[3,1,32,320]{3,2,1,0:T(8,128)S(1)}, f32[3,1,32,320]{3,2,1,0:T(8,128)S(1)}, u32[]{:S(2)}, u32[]{:S(2)}) %collective-permute-start.8) | collective-permute-done | bytes 122912 | tf_op jit(solution)/shard_map/ppermute | solution.py:19
  54.4 2.2 %collective-permute-start.10 = (f32[3,14,1,320]{3,2,1,0:T(1,128)S(1)}, f32[3,14,1,320]{3,2,1,0:T(1,128)S(1)}, u32[]{:S(2)}, u32[]{:S(2)}) collective-permute-start(f32[3,14,1,320]{3,2,1,0:T(1,128)S(1)} %get-tuple-element.17), channel_id=1, source_target_pairs={{0,1},{1,2},{2,3},{3,0},{4,5},{5,6},{6,7},{7,4},{8,9},{9,10},{10,1... | collective-permute-start | bytes 161288 | tf_op jit(solution)/shard_map/ppermute | solution.py:19
  56.6 1.3 collective-permute-done.10
  57.9 2.4 %collective-permute-done.11 = f32[3,14,1,320]{3,2,1,0:T(1,128)S(1)} collective-permute-done((f32[3,14,1,320]{3,2,1,0:T(1,128)S(1)}, f32[3,14,1,320]{3,2,1,0:T(1,128)S(1)}, u32[]{:S(2)}, u32[]{:S(2)}) %collective-permute-start.11) | collective-permute-done | bytes 53792 | tf_op jit(solution)/shard_map/ppermute | solution.py:20
  60.8 2.6 %add_select_fusion.2 = f32[3,12,32,320]{3,2,1,0:T(8,128)S(1)} fusion(f32[3,14,34,320]{3,2,1,0:T(8,128)S(1)} %maximum_select_fusion.1, f32[12,32,320]{2,1,0:T(8,128)S(1)} %get-tuple-element.4, f32[12,32,320]{2,1,0:T(8,128)S(1)} %get-tuple-element.10, f32[12,32,320]{2,1,0:T(8,128)S(1)} %get-tuple-element.9, f32[12,32,320]{2,1,0:T(8,128)S(1)} %get-tuple-element.8, ...), kind=kLoop, calls=%fused_computation.2 | loop fusion | flops 5898240 | bytes 17178624 | tf_op jit(solution)/shard_map/jit(_where)/select_n | solution.py:56
  63.4 9.3 %collective-permute-start.13 = (f32[3,1,32,320]{3,2,1,0:T(8,128)S(1)}, f32[3,1,32,320]{3,2,1,0:T(8,128)S(1)}, u32[]{:S(2)}, u32[]{:S(2)}) collective-permute-start(f32[3,1,32,320]{3,2,1,0:T(8,128)S(1)} %get-tuple-element.26), channel_id=1, source_target_pairs={{4,0},{8,4},{12,8},{16,12},{20,16},{24,20},{28,24},{32,28},{36,32}... | collective-permute-start | bytes 368648 | tf_op jit(solution)/shard_map/ppermute | solution.py:20
  72.8 3.8 %collective-permute-done.12 = f32[3,1,32,320]{3,2,1,0:T(8,128)S(1)} collective-permute-done((f32[3,1,32,320]{3,2,1,0:T(8,128)S(1)}, f32[3,1,32,320]{3,2,1,0:T(8,128)S(1)}, u32[]{:S(2)}, u32[]{:S(2)}) %collective-permute-start.12) | collective-permute-done | bytes 122912 | tf_op jit(solution)/shard_map/ppermute | solution.py:19
  77.8 1.1 collective-permute-done.14
  78.8 2.5 %collective-permute-done.15 = f32[3,14,1,320]{3,2,1,0:T(1,128)S(1)} collective-permute-done((f32[3,14,1,320]{3,2,1,0:T(1,128)S(1)}, f32[3,14,1,320]{3,2,1,0:T(1,128)S(1)}, u32[]{:S(2)}, u32[]{:S(2)}) %collective-permute-start.15) | collective-permute-done | bytes 53792 | tf_op jit(solution)/shard_map/ppermute | solution.py:20
  81.8 2.6 %add_select_fusion.1 = f32[3,12,32,320]{3,2,1,0:T(8,128)S(1)} fusion(f32[3,14,34,320]{3,2,1,0:T(8,128)S(1)} %maximum_select_fusion.2, f32[12,32,320]{2,1,0:T(8,128)S(1)} %get-tuple-element.4, f32[12,32,320]{2,1,0:T(8,128)S(1)} %get-tuple-element.10, f32[12,32,320]{2,1,0:T(8,128)S(1)} %get-tuple-element.9, f32[12,32,320]{2,1,0:T(8,128)S(1)} %get-tuple-element.8, ...), kind=kLoop, calls=%fused_computation.1 | loop fusion | flops 5898240 | bytes 17178624 | tf_op jit(solution)/shard_map/jit(_where)/select_n | solution.py:56
  84.5 7.8 %collective-permute-start.17 = (f32[3,1,32,320]{3,2,1,0:T(8,128)S(1)}, f32[3,1,32,320]{3,2,1,0:T(8,128)S(1)}, u32[]{:S(2)}, u32[]{:S(2)}) collective-permute-start(f32[3,1,32,320]{3,2,1,0:T(8,128)S(1)} %get-tuple-element.24), channel_id=1, source_target_pairs={{4,0},{8,4},{12,8},{16,12},{20,16},{24,20},{28,24},{32,28},{36,32}... | collective-permute-start | bytes 368648 | tf_op jit(solution)/shard_map/ppermute | solution.py:20
  92.3 4.2 %collective-permute-done.16 = f32[3,1,32,320]{3,2,1,0:T(8,128)S(1)} collective-permute-done((f32[3,1,32,320]{3,2,1,0:T(8,128)S(1)}, f32[3,1,32,320]{3,2,1,0:T(8,128)S(1)}, u32[]{:S(2)}, u32[]{:S(2)}) %collective-permute-start.16) | collective-permute-done | bytes 122912 | tf_op jit(solution)/shard_map/ppermute | solution.py:19
  98.0 2.9 %collective-permute-done.19 = f32[3,14,1,320]{3,2,1,0:T(1,128)S(1)} collective-permute-done((f32[3,14,1,320]{3,2,1,0:T(1,128)S(1)}, f32[3,14,1,320]{3,2,1,0:T(1,128)S(1)}, u32[]{:S(2)}, u32[]{:S(2)}) %collective-permute-start.19) | collective-permute-done | bytes 53792 | tf_op jit(solution)/shard_map/ppermute | solution.py:20
  101.3 2.6 %add_select_fusion = f32[3,12,32,320]{3,2,1,0:T(8,128)S(1)} fusion(f32[3,14,34,320]{3,2,1,0:T(8,128)S(1)} %maximum_select_fusion.3, f32[12,32,320]{2,1,0:T(8,128)S(1)} %get-tuple-element.4, f32[12,32,320]{2,1,0:T(8,128)S(1)} %get-tuple-element.10, f32[12,32,320]{2,1,0:T(8,128)S(1)} %get-tuple-element.9, f32[12,32,320]{2,1,0:T(8,128)S(1)} %get-tuple-element.8, ...), kind=kLoop, calls=%fused_computation | loop fusion | flops 5898240 | bytes 17178624 | tf_op jit(solution)/shard_map/jit(_where)/select_n | solution.py:56
  104.0 7.3 %collective-permute-start.21 = (f32[3,1,32,320]{3,2,1,0:T(8,128)S(1)}, f32[3,1,32,320]{3,2,1,0:T(8,128)S(1)}, u32[]{:S(2)}, u32[]{:S(2)}) collective-permute-start(f32[3,1,32,320]{3,2,1,0:T(8,128)S(1)} %get-tuple-element.22), channel_id=1, source_target_pairs={{4,0},{8,4},{12,8},{16,12},{20,16},{24,20},{28,24},{32,28},{36,32}... | collective-permute-start | bytes 368648 | tf_op jit(solution)/shard_map/ppermute | solution.py:20
  111.4 3.7 %collective-permute-done.20 = f32[3,1,32,320]{3,2,1,0:T(8,128)S(1)} collective-permute-done((f32[3,1,32,320]{3,2,1,0:T(8,128)S(1)}, f32[3,1,32,320]{3,2,1,0:T(8,128)S(1)}, u32[]{:S(2)}, u32[]{:S(2)}) %collective-permute-start.20) | collective-permute-done | bytes 122912 | tf_op jit(solution)/shard_map/ppermute | solution.py:19
  117.0 3.2 %collective-permute-done.23 = f32[3,14,1,320]{3,2,1,0:T(1,128)S(1)} collective-permute-done((f32[3,14,1,320]{3,2,1,0:T(1,128)S(1)}, f32[3,14,1,320]{3,2,1,0:T(1,128)S(1)}, u32[]{:S(2)}, u32[]{:S(2)}) %collective-permute-start.23) | collective-permute-done | bytes 53792 | tf_op jit(solution)/shard_map/ppermute | solution.py:20
  120.7 3.1 %fusion.51 = f32[]{:T(128)} fusion(f32[3,14,34,320]{3,2,1,0:T(8,128)S(1)} %maximum_select_fusion.4, f32[12,32,320]{2,1,0:T(8,128)S(1)} %get-tuple-element.4, f32[12,32,320]{2,1,0:T(8,128)S(1)} %get-tuple-element.10, f32[12,32,320]{2,1,0:T(8,128)S(1)} %get-tuple-element.9, f32[12,32,320]{2,1,0:T(8,128)S(1)} %get-tuple-element.8, ...), kind=kLoop, calls=%fused_computation.90 | loop fusion | flops 5898239 | bytes 15704068 | tf_op jit(solution)/shard_map/reduce_sum | solution.py:104
  123.8 77.5 %psum.7 = f32[]{:T(128)} all-reduce(f32[]{:T(128)} %fusion.51), channel_id=1, replica_groups=mesh['theta'=64,'rad'=4] {'theta','rad'}, use_global_device_ids=true, to_apply=%region_1.2 | all-reduce | flops 1 | bytes 8 | tf_op jit(solution)/shard_map/psum | solution.py:104
  (63 shorter events, 10.5 us)
Async XLA Ops:
  0.6 22.5 %copy-start.2 = (f32[12,32,320]{2,1,0:T(8,128)S(1)}, f32[12,32,320]{2,1,0:T(8,128)}, u32[]{:S(2)}) copy-start(f32[12,32,320]{2,1,0:T(8,128)} %param.4) | copy-start | bytes 1474564
  1.5 21.7 %collective-permute-start.5 = (f32[1,32,320]{2,1,0:T(8,128)S(1)}, f32[1,32,320]{2,1,0:T(8,128)S(1)}, u32[]{:S(2)}, u32[]{:S(2)}) collective-permute-start(f32[1,32,320]{2,1,0:T(8,128)S(1)} %get-tuple-element.35), channel_id=1, source_target_pairs={{4,0},{8,4},{12,8},{16,12},{20,16},{24,20},{28,24},{32,28},{36,32}... | collective-permute-start | bytes 122888 | tf_op jit(solution)/shard_map/ppermute | solution.py:20
  12.8 10.3 %collective-permute-start.4 = (f32[1,32,320]{2,1,0:T(8,128)S(1)}, f32[1,32,320]{2,1,0:T(8,128)S(1)}, u32[]{:S(2)}, u32[]{:S(2)}) collective-permute-start(f32[1,32,320]{2,1,0:T(8,128)S(1)} %get-tuple-element.36), channel_id=1, source_target_pairs={{0,4},{4,8},{8,12},{12,16},{16,20},{20,24},{24,28},{28,32},{32,36}... | collective-permute-start | bytes 122888 | tf_op jit(solution)/shard_map/ppermute | solution.py:19
  13.8 17.1 %collective-permute-start.1 = (f32[3,1,32,320]{3,2,1,0:T(8,128)S(1)}, f32[3,1,32,320]{3,2,1,0:T(8,128)S(1)}, u32[]{:S(2)}, u32[]{:S(2)}) collective-permute-start(f32[3,1,32,320]{3,2,1,0:T(8,128)S(1)} %get-tuple-element.29), channel_id=1, source_target_pairs={{4,0},{8,4},{12,8},{16,12},{20,16},{24,20},{28,24},{32,28},{36,32}... | collective-permute-start | bytes 368648 | tf_op jit(solution)/shard_map/ppermute | solution.py:20
  21.1 9.7 %collective-permute-start = (f32[3,1,32,320]{3,2,1,0:T(8,128)S(1)}, f32[3,1,32,320]{3,2,1,0:T(8,128)S(1)}, u32[]{:S(2)}, u32[]{:S(2)}) collective-permute-start(f32[3,1,32,320]{3,2,1,0:T(8,128)S(1)} %get-tuple-element.30), channel_id=1, source_target_pairs={{0,4},{4,8},{8,12},{12,16},{16,20},{20,24},{24,28},{28,32},{32,36}... | collective-permute-start | bytes 368648 | tf_op jit(solution)/shard_map/ppermute | solution.py:19
  23.3 2.8 %collective-permute-start.6 = (f32[14,1,320]{2,1,0:T(1,128)S(1)}, f32[14,1,320]{2,1,0:T(1,128)S(1)}, u32[]{:S(2)}, u32[]{:S(2)}) collective-permute-start(f32[14,1,320]{2,1,0:T(1,128)S(1)} %get-tuple-element.33), channel_id=1, source_target_pairs={{0,1},{1,2},{2,3},{3,0},{4,5},{5,6},{6,7},{7,4},{8,9},{9,10},{10,1... | collective-permute-start | bytes 53768 | tf_op jit(solution)/shard_map/ppermute | solution.py:19
  25.1 3.2 %collective-permute-start.7 = (f32[14,1,320]{2,1,0:T(1,128)S(1)}, f32[14,1,320]{2,1,0:T(1,128)S(1)}, u32[]{:S(2)}, u32[]{:S(2)}) collective-permute-start(f32[14,1,320]{2,1,0:T(1,128)S(1)} %get-tuple-element.34), channel_id=1, source_target_pairs={{1,0},{2,1},{3,2},{0,3},{5,4},{6,5},{7,6},{4,7},{9,8},{10,9},{11,1... | collective-permute-start | bytes 53768 | tf_op jit(solution)/shard_map/ppermute | solution.py:20
  28.5 2.3 %copy-start.1 = (f32[3,12,32,320]{3,2,1,0:T(8,128)S(1)}, f32[3,12,32,320]{3,2,1,0:T(8,128)}, u32[]{:S(2)}) copy-start(f32[3,12,32,320]{3,2,1,0:T(8,128)} %param.3) | copy-start | bytes 4423684
  31.1 7.9 %collective-permute-start.2 = (f32[3,14,1,320]{3,2,1,0:T(1,128)S(1)}, f32[3,14,1,320]{3,2,1,0:T(1,128)S(1)}, u32[]{:S(2)}, u32[]{:S(2)}) collective-permute-start(f32[3,14,1,320]{3,2,1,0:T(1,128)S(1)} %get-tuple-element.19), channel_id=1, source_target_pairs={{0,1},{1,2},{2,3},{3,0},{4,5},{5,6},{6,7},{7,4},{8,9},{9,10},{10,1... | collective-permute-start | bytes 161288 | tf_op jit(solution)/shard_map/ppermute | solution.py:19
  34.1 6.3 %collective-permute-start.3 = (f32[3,14,1,320]{3,2,1,0:T(1,128)S(1)}, f32[3,14,1,320]{3,2,1,0:T(1,128)S(1)}, u32[]{:S(2)}, u32[]{:S(2)}) collective-permute-start(f32[3,14,1,320]{3,2,1,0:T(1,128)S(1)} %get-tuple-element.20), channel_id=1, source_target_pairs={{1,0},{2,1},{3,2},{0,3},{5,4},{6,5},{7,6},{4,7},{9,8},{10,9},{11,1... | collective-permute-start | bytes 161288 | tf_op jit(solution)/shard_map/ppermute | solution.py:20
  43.5 10.8 %collective-permute-start.8 = (f32[3,1,32,320]{3,2,1,0:T(8,128)S(1)}, f32[3,1,32,320]{3,2,1,0:T(8,128)S(1)}, u32[]{:S(2)}, u32[]{:S(2)}) collective-permute-start(f32[3,1,32,320]{3,2,1,0:T(8,128)S(1)} %get-tuple-element.27), channel_id=1, source_target_pairs={{0,4},{4,8},{8,12},{12,16},{16,20},{20,24},{24,28},{28,32},{32,36}... | collective-permute-start | bytes 368648 | tf_op jit(solution)/shard_map/ppermute | solution.py:19
  43.6 10.7 %collective-permute-start.9 = (f32[3,1,32,320]{3,2,1,0:T(8,128)S(1)}, f32[3,1,32,320]{3,2,1,0:T(8,128)S(1)}, u32[]{:S(2)}, u32[]{:S(2)}) collective-permute-start(f32[3,1,32,320]{3,2,1,0:T(8,128)S(1)} %get-tuple-element.28), channel_id=1, source_target_pairs={{4,0},{8,4},{12,8},{16,12},{20,16},{24,20},{28,24},{32,28},{36,32}... | collective-permute-start | bytes 368648 | tf_op jit(solution)/shard_map/ppermute | solution.py:20
  54.4 3.5 %collective-permute-start.10 = (f32[3,14,1,320]{3,2,1,0:T(1,128)S(1)}, f32[3,14,1,320]{3,2,1,0:T(1,128)S(1)}, u32[]{:S(2)}, u32[]{:S(2)}) collective-permute-start(f32[3,14,1,320]{3,2,1,0:T(1,128)S(1)} %get-tuple-element.17), channel_id=1, source_target_pairs={{0,1},{1,2},{2,3},{3,0},{4,5},{5,6},{6,7},{7,4},{8,9},{9,10},{10,1... | collective-permute-start | bytes 161288 | tf_op jit(solution)/shard_map/ppermute | solution.py:19
  56.6 3.7 %collective-permute-start.11 = (f32[3,14,1,320]{3,2,1,0:T(1,128)S(1)}, f32[3,14,1,320]{3,2,1,0:T(1,128)S(1)}, u32[]{:S(2)}, u32[]{:S(2)}) collective-permute-start(f32[3,14,1,320]{3,2,1,0:T(1,128)S(1)} %get-tuple-element.18), channel_id=1, source_target_pairs={{1,0},{2,1},{3,2},{0,3},{5,4},{6,5},{7,6},{4,7},{9,8},{10,9},{11,1... | collective-permute-start | bytes 161288 | tf_op jit(solution)/shard_map/ppermute | solution.py:20
  63.3 13.2 %collective-permute-start.12 = (f32[3,1,32,320]{3,2,1,0:T(8,128)S(1)}, f32[3,1,32,320]{3,2,1,0:T(8,128)S(1)}, u32[]{:S(2)}, u32[]{:S(2)}) collective-permute-start(f32[3,1,32,320]{3,2,1,0:T(8,128)S(1)} %get-tuple-element.25), channel_id=1, source_target_pairs={{0,4},{4,8},{8,12},{12,16},{16,20},{20,24},{24,28},{28,32},{32,36}... | collective-permute-start | bytes 368648 | tf_op jit(solution)/shard_map/ppermute | solution.py:19
  63.4 13.2 %collective-permute-start.13 = (f32[3,1,32,320]{3,2,1,0:T(8,128)S(1)}, f32[3,1,32,320]{3,2,1,0:T(8,128)S(1)}, u32[]{:S(2)}, u32[]{:S(2)}) collective-permute-start(f32[3,1,32,320]{3,2,1,0:T(8,128)S(1)} %get-tuple-element.26), channel_id=1, source_target_pairs={{4,0},{8,4},{12,8},{16,12},{20,16},{24,20},{28,24},{32,28},{36,32}... | collective-permute-start | bytes 368648 | tf_op jit(solution)/shard_map/ppermute | solution.py:20
  76.7 2.2 %collective-permute-start.14 = (f32[3,14,1,320]{3,2,1,0:T(1,128)S(1)}, f32[3,14,1,320]{3,2,1,0:T(1,128)S(1)}, u32[]{:S(2)}, u32[]{:S(2)}) collective-permute-start(f32[3,14,1,320]{3,2,1,0:T(1,128)S(1)} %get-tuple-element.15), channel_id=1, source_target_pairs={{0,1},{1,2},{2,3},{3,0},{4,5},{5,6},{6,7},{7,4},{8,9},{9,10},{10,1... | collective-permute-start | bytes 161288 | tf_op jit(solution)/shard_map/ppermute | solution.py:19
  77.5 3.8 %collective-permute-start.15 = (f32[3,14,1,320]{3,2,1,0:T(1,128)S(1)}, f32[3,14,1,320]{3,2,1,0:T(1,128)S(1)}, u32[]{:S(2)}, u32[]{:S(2)}) collective-permute-start(f32[3,14,1,320]{3,2,1,0:T(1,128)S(1)} %get-tuple-element.16), channel_id=1, source_target_pairs={{1,0},{2,1},{3,2},{0,3},{5,4},{6,5},{7,6},{4,7},{9,8},{10,9},{11,1... | collective-permute-start | bytes 161288 | tf_op jit(solution)/shard_map/ppermute | solution.py:20
  84.4 12.0 %collective-permute-start.16 = (f32[3,1,32,320]{3,2,1,0:T(8,128)S(1)}, f32[3,1,32,320]{3,2,1,0:T(8,128)S(1)}, u32[]{:S(2)}, u32[]{:S(2)}) collective-permute-start(f32[3,1,32,320]{3,2,1,0:T(8,128)S(1)} %get-tuple-element.23), channel_id=1, source_target_pairs={{0,4},{4,8},{8,12},{12,16},{16,20},{20,24},{24,28},{28,32},{32,36}... | collective-permute-start | bytes 368648 | tf_op jit(solution)/shard_map/ppermute | solution.py:19
  84.5 12.0 %collective-permute-start.17 = (f32[3,1,32,320]{3,2,1,0:T(8,128)S(1)}, f32[3,1,32,320]{3,2,1,0:T(8,128)S(1)}, u32[]{:S(2)}, u32[]{:S(2)}) collective-permute-start(f32[3,1,32,320]{3,2,1,0:T(8,128)S(1)} %get-tuple-element.24), channel_id=1, source_target_pairs={{4,0},{8,4},{12,8},{16,12},{20,16},{24,20},{28,24},{32,28},{36,32}... | collective-permute-start | bytes 368648 | tf_op jit(solution)/shard_map/ppermute | solution.py:20
  96.6 1.4 collective-permute-start.18
  96.7 4.2 %collective-permute-start.19 = (f32[3,14,1,320]{3,2,1,0:T(1,128)S(1)}, f32[3,14,1,320]{3,2,1,0:T(1,128)S(1)}, u32[]{:S(2)}, u32[]{:S(2)}) collective-permute-start(f32[3,14,1,320]{3,2,1,0:T(1,128)S(1)} %get-tuple-element.14), channel_id=1, source_target_pairs={{1,0},{2,1},{3,2},{0,3},{5,4},{6,5},{7,6},{4,7},{9,8},{10,9},{11,1... | collective-permute-start | bytes 161288 | tf_op jit(solution)/shard_map/ppermute | solution.py:20
  103.9 16.8 %copy-start = (f32[3,12,32,320]{3,2,1,0:T(8,128)}, f32[3,12,32,320]{3,2,1,0:T(8,128)S(1)}, u32[]{:S(2)}) copy-start(f32[3,12,32,320]{3,2,1,0:T(8,128)S(1)} %add_select_fusion) | copy-start | bytes 4423684
  103.9 11.1 %collective-permute-start.20 = (f32[3,1,32,320]{3,2,1,0:T(8,128)S(1)}, f32[3,1,32,320]{3,2,1,0:T(8,128)S(1)}, u32[]{:S(2)}, u32[]{:S(2)}) collective-permute-start(f32[3,1,32,320]{3,2,1,0:T(8,128)S(1)} %get-tuple-element.21), channel_id=1, source_target_pairs={{0,4},{4,8},{8,12},{12,16},{16,20},{20,24},{24,28},{28,32},{32,36}... | collective-permute-start | bytes 368648 | tf_op jit(solution)/shard_map/ppermute | solution.py:19
  104.0 11.0 %collective-permute-start.21 = (f32[3,1,32,320]{3,2,1,0:T(8,128)S(1)}, f32[3,1,32,320]{3,2,1,0:T(8,128)S(1)}, u32[]{:S(2)}, u32[]{:S(2)}) collective-permute-start(f32[3,1,32,320]{3,2,1,0:T(8,128)S(1)} %get-tuple-element.22), channel_id=1, source_target_pairs={{4,0},{8,4},{12,8},{16,12},{20,16},{24,20},{28,24},{32,28},{36,32}... | collective-permute-start | bytes 368648 | tf_op jit(solution)/shard_map/ppermute | solution.py:20
  115.1 1.9 collective-permute-start.22
  115.6 4.6 %collective-permute-start.23 = (f32[3,14,1,320]{3,2,1,0:T(1,128)S(1)}, f32[3,14,1,320]{3,2,1,0:T(1,128)S(1)}, u32[]{:S(2)}, u32[]{:S(2)}) collective-permute-start(f32[3,14,1,320]{3,2,1,0:T(1,128)S(1)} %get-tuple-element.12), channel_id=1, source_target_pairs={{1,0},{2,1},{3,2},{0,3},{5,4},{6,5},{7,6},{4,7},{9,8},{10,9},{11,1... | collective-permute-start | bytes 161288 | tf_op jit(solution)/shard_map/ppermute | solution.py:20
where the time goes:
time: 203 us
  blocking collectives  77.5 us (38%)
  starting transfers between devices  60.9 us (30%)
  waiting for transfers between devices  40.3 us (20%)
  other arithmetic  19.1 us (9%)
  between operations  2.8 us (1%)
  local copies, waits for them, and re-layouts  2.48 us (1%)
    psum x1, blocking collectives, shards(): squared = lax.psum(jnp.sum(residual * residual), ('theta', 'rad'))  77.5 us
    ppermute x12, starting transfers between devices, with_halo(): after = lax.ppermute(initial, axis, down)  52.1 us
    ppermute x12, waiting for transfers between devices, with_halo(): before = lax.ppermute(last, axis, up)  25.6 us
    ppermute x12, waiting for transfers between devices, with_halo(): after = lax.ppermute(initial, axis, down)  14.7 us
    select_n x4, other arithmetic, relax(): return (jnp.where(chosen, updated, center), average - center)  10.2 us
    ppermute x12, starting transfers between devices, with_halo(): before = lax.ppermute(last, axis, up)  8.73 us
  transfers between devices with their start and end apart: 24, of which 17 were waited for; matrix products, arithmetic and copies ran while one was open for 2% of the time, Pallas kernels for 0%

commit v1 on v0

v1 whole, which is shorter than its diff:
```python
import functools

import jax
import jax.numpy as jnp
from jax import lax
from jax.experimental import pallas as pl
from jax.experimental.pallas import tpu as pltpu
from jax.sharding import PartitionSpec as P

MESH = pl.DeviceIdType.MESH
F32 = jnp.float32
LANES = 128
OFF = 8
NAMES = ("self", "in", "out", "rp", "rm", "ap", "am")
SELF, IN, OUT, RP, RM, AP, AM = range(7)


def iota(dim):
    return lax.broadcasted_iota(jnp.int32, (8, LANES), dim)


def kernel(
    cfg, d_hbm, s_hbm, w_hbm, out_hbm, norm_ref,
    raw_d, raw_s, raw_w, field, stiff, weight, stage, land, edge_s, part, gather,
    load_sem, out_sem, th_send, th_recv, es_send, es_recv, rd_send, rd_recv, rs_send, rs_recv, ar_send, ar_recv,
):
    n_theta, n_rad, pairs, rows, cols, tiles, levels, count = cfg
    t, r = lax.axis_index("theta"), lax.axis_index("rad")
    tile_rows = rows // 8
    last_lanes = cols - (tiles - 1) * LANES
    nxt, prv = (lax.rem(t + 1, n_theta), r), (lax.rem(t + n_theta - 1, n_theta), r)
    above, below = (t, jnp.minimum(r + 1, n_rad - 1)), (t, jnp.maximum(r - 1, 0))
    has_above, has_below = r < n_rad - 1, r > 0

    loads = [
        pltpu.make_async_copy(s_hbm, raw_s, load_sem.at[0]),
        pltpu.make_async_copy(w_hbm, raw_w, load_sem.at[1]),
        pltpu.make_async_copy(d_hbm, raw_d, load_sem.at[2]),
    ]
    for c in loads:
        c.start()

    groups = [level(t, r) for level in levels]
    barrier = pltpu.get_barrier_semaphore()
    greet = [nxt, prv] + [p for g in groups for p in g]
    for p in greet:
        pl.semaphore_signal(barrier, inc=1, device_id=p, device_id_type=MESH)

    even = (iota(0) + iota(1)) % 2 == 0
    first_lane, last_lane = iota(1) == 0, iota(1) == LANES - 1
    inside = iota(1) < last_lanes
    at_first_col, at_last_col = iota(1) == 0, iota(1) == last_lanes - 1

    def raw_tile(ref, lead, i, q):
        if q < tiles - 1:
            return ref[(*lead, pl.ds(8 * i, 8), pl.ds(q * LANES, LANES))]
        x = ref[(*lead, pl.ds(8 * i, 8), pl.ds(q * LANES, last_lanes))]
        if last_lanes == LANES:
            return x
        return jnp.concatenate([x, jnp.zeros((8, LANES - last_lanes), x.dtype)], axis=1)

    def at(i, shift=0):
        return pl.ds(OFF + 8 * i + shift, 8)

    zero_row = jnp.zeros((1, LANES), F32)
    loads[0].wait()

    def pack_s(k, _):
        for i in range(tile_rows):
            for q in range(tiles):
                a, b = raw_tile(raw_s, (2 * k,), i, q), raw_tile(raw_s, (2 * k + 1,), i, q)
                stiff[0, k + 1, q, at(i), :] = jnp.where(even, a, b)
                stiff[1, k + 1, q, at(i), :] = jnp.where(even, b, a)
        return 0

    lax.fori_loop(0, pairs, pack_s, 0)
    loads[2].wait()

    def pack_d(j, _):
        c, k = j // pairs, j % pairs
        for i in range(tile_rows):
            for q in range(tiles):
                a, b = raw_tile(raw_d, (c, 2 * k), i, q), raw_tile(raw_d, (c, 2 * k + 1), i, q)
                field[0, c, k + 1, q, at(i), :] = jnp.where(even, a, b)
                field[1, c, k + 1, q, at(i), :] = jnp.where(even, b, a)
        return 0

    lax.fori_loop(0, 3 * pairs, pack_d, 0)
    loads[1].wait()

    @pl.when(jnp.logical_not(has_below))
    def _():
        for colour in range(2):
            for k in range(pairs):
                for q in range(tiles):
                    stiff[colour, k + 1, q, pl.ds(OFF - 1, 1), :] = zero_row
                    for c in range(3):
                        field[colour, c, k + 1, q, pl.ds(OFF - 1, 1), :] = zero_row

    @pl.when(jnp.logical_not(has_above))
    def _():
        for colour in range(2):
            for k in range(pairs):
                for q in range(tiles):
                    stiff[colour, k + 1, q, pl.ds(OFF + rows, 1), :] = zero_row
                    for c in range(3):
                        field[colour, c, k + 1, q, pl.ds(OFF + rows, 1), :] = zero_row

    def theta_copies(n):
        return [
            pltpu.make_async_remote_copy(
                stage.at[n, side], land.at[n, 1 - side], th_send.at[n, side], th_recv.at[n, 1 - side],
                device_id=p, device_id_type=MESH,
            )
            for side, p in ((0, prv), (1, nxt))
        ]

    def send_theta(n, colour):
        for side in range(2):
            k = 1 if side == 0 else pairs
            keep = even if side == colour else jnp.logical_not(even)
            for c in range(3):
                for q in range(tiles):
                    for h in range(tile_rows // 2):
                        a = field[colour, c, k, q, at(2 * h), :]
                        b = field[colour, c, k, q, at(2 * h + 1), :]
                        stage[n, side, c, q, pl.ds(8 * h, 8), :] = jnp.where(keep, a, pltpu.roll(b, 1, 0))
        for copy in theta_copies(n):
            copy.start()

    def take_theta(n, colour):
        for copy in theta_copies(n):
            copy.wait_recv()
        for side in range(2):
            k = 0 if side == 0 else pairs + 1
            for c in range(3):
                for q in range(tiles):
                    for h in range(tile_rows // 2):
                        x = land[n, side, c, q, pl.ds(8 * h, 8), :]
                        field[colour, c, k, q, at(2 * h), :] = x
                        field[colour, c, k, q, at(2 * h + 1), :] = pltpu.roll(x, 7, 0)

    own = pl.ds(1, pairs)

    def rad_copy(ref, lead, up, send, recv):
        src, dst = (OFF + rows - 1, OFF - 1) if up else (OFF, OFF + rows)
        return pltpu.make_async_remote_copy(
            ref.at[(*lead, own, slice(None), pl.ds(src, 1))], ref.at[(*lead, own, slice(None), pl.ds(dst, 1))],
            send, recv, device_id=above if up else below, device_id_type=MESH,
        )

    def field_copy(n, colour, up):
        return rad_copy(field, (colour, slice(None)), up, rd_send.at[n, up], rd_recv.at[n, up])

    def stiff_copy(colour, up):
        return rad_copy(stiff, (colour,), up, rs_send.at[colour, up], rs_recv.at[colour, up])

    def send_rad(copy):
        @pl.when(has_above)
        def _():
            copy(1).start()

        @pl.when(has_below)
        def _():
            copy(0).start()

    def take_rad(copy):
        @pl.when(has_below)
        def _():
            copy(1).wait_recv()

        @pl.when(has_above)
        def _():
            copy(0).wait_recv()

    def drain_rad(copy):
        @pl.when(has_above)
        def _():
            copy(1).wait_send()

        @pl.when(has_below)
        def _():
            copy(0).wait_send()

    edge_copies = [
        pltpu.make_async_remote_copy(
            raw_s.at[0 if side == 0 else 2 * pairs - 1], edge_s.at[1 - side], es_send.at[side], es_recv.at[1 - side],
            device_id=p, device_id_type=MESH,
        )
        for side, p in ((0, prv), (1, nxt))
    ]

    pl.semaphore_wait(barrier, len(greet))
    for copy in edge_copies:
        copy.start()
    for colour in range(2):
        send_rad(functools.partial(stiff_copy, colour))
    send_theta(0, 1)
    send_rad(functools.partial(field_copy, 0, 1))

    def beside(v, w, side):
        out = []
        for q in range(tiles):
            if side:
                x = pltpu.roll(v[q], LANES - 1, 1)
                if q < tiles - 1:
                    x = jnp.where(last_lane, pltpu.roll(v[q + 1], LANES - 1, 1), x)
            else:
                x = pltpu.roll(v[q], 1, 1)
                if q > 0:
                    x = jnp.where(first_lane, pltpu.roll(v[q - 1], 1, 1), x)
            out.append(x)
        return out

    def outer(colour, before, after):
        return jnp.where(even, before, after) if colour == 0 else jnp.where(even, after, before)

    def make_weights(colour, k):
        other = 1 - colour
        for i in range(tile_rows):
            mid = [stiff[other, k + 1, q, at(i), :] for q in range(tiles)]
            forth, back = beside(mid, None, 1), beside(mid, None, 0)
            for q in range(tiles):
                s = stiff[colour, k + 1, q, at(i), :]
                faces = [None] * 7
                faces[IN] = s + mid[q]
                faces[OUT] = s + outer(colour, stiff[other, k, q, at(i), :], stiff[other, k + 2, q, at(i), :])
                faces[RP] = s + stiff[other, k + 1, q, at(i, 1), :]
                faces[RM] = s + stiff[other, k + 1, q, at(i, -1), :]
                ap, am = forth[q], back[q]
                if q == tiles - 1:
                    ap = jnp.where(at_last_col, s, ap)
                if q == 0:
                    am = jnp.where(at_first_col, s, am)
                faces[AP], faces[AM] = s + ap, s + am
                total = faces[IN] + faces[OUT] + (faces[RP] + faces[RM]) + (faces[AP] + faces[AM])
                wa, wb = raw_tile(raw_w, (2 * k,), i, q), raw_tile(raw_w, (2 * k + 1,), i, q)
                fixed = (jnp.where(even, wa, wb) if colour == 0 else jnp.where(even, wb, wa)) != 0
                if q == tiles - 1 and last_lanes < LANES:
                    fixed = jnp.logical_or(fixed, jnp.logical_not(inside))
                scale = jnp.where(fixed, 0.0, 1.5 / total)
                put = pl.ds(8 * i, 8)
                weight[colour, SELF, k, q, put, :] = jnp.where(fixed, 1.0, -0.5)
                for f in (IN, OUT, RP, RM, AP, AM):
                    w = faces[f] * scale
                    if f == AP and q == tiles - 1:
                        w = jnp.where(at_last_col, 0.0, w)
                    if f == AM and q == 0:
                        w = jnp.where(at_first_col, 0.0, w)
                    weight[colour, f, k, q, put, :] = w

    def half(colour, k, mode, acc):
        other = 1 - colour
        for i in range(tile_rows):
            put = pl.ds(8 * i, 8)
            w = [[weight[colour, f, k, q, put, :] for q in range(tiles)] for f in range(7)]
            for c in range(3):
                mid = [field[other, c, k + 1, q, at(i), :] for q in range(tiles)]
                forth, back = beside(mid, None, 1), beside(mid, None, 0)
                for q in range(tiles):
                    far = outer(colour, field[other, c, k, q, at(i), :], field[other, c, k + 2, q, at(i), :])
                    old = field[colour, c, k + 1, q, at(i), :]
                    new = w[SELF][q] * old + w[IN][q] * mid[q] + w[OUT][q] * far
                    new = new + w[RP][q] * field[other, c, k + 1, q, at(i, 1), :]
                    new = new + w[RM][q] * field[other, c, k + 1, q, at(i, -1), :]
                    new = new + w[AP][q] * forth[q] + w[AM][q] * back[q]
                    if mode < 2:
                        field[colour, c, k + 1, q, at(i), :] = new
                    if mode > 0:
                        change = new - old
                        acc = acc + change * change
        return acc

    def over(lo, hi, fn, acc):
        return lax.fori_loop(lo, hi, fn, acc)

    zero = jnp.zeros((8, LANES), F32)
    sums = [zero, zero]
    for n in range(5):
        colour, seen = n % 2, 1 - n % 2
        mode = (0, 0, 0, 1, 2)[n]
        if n > 0:
            drain_rad(functools.partial(field_copy, n - 1, colour))
        if n == 0:
            for col in range(2):
                take_rad(functools.partial(stiff_copy, col))

            def inner_weights(k, _):
                make_weights(0, k)
                make_weights(1, k)
                return 0

            lax.fori_loop(1, pairs - 1, inner_weights, 0)
        take_rad(functools.partial(field_copy, n, seen))
        acc = over(1, pairs - 1, lambda k, a: half(colour, k, mode, a), zero)
        if n == 0:
            for copy in edge_copies:
                copy.wait_recv()
            for side in range(2):
                for i in range(tile_rows):
                    for q in range(tiles):
                        x = raw_tile(edge_s, (side,), i, q)
                        k = 0 if side == 0 else pairs + 1
                        stiff[0, k, q, at(i), :] = x
                        stiff[1, k, q, at(i), :] = x

            def outer_weights(j, _):
                make_weights(0, j * (pairs - 1))
                make_weights(1, j * (pairs - 1))
                return 0

            lax.fori_loop(0, 2, outer_weights, 0)
        take_theta(n, seen)
        acc = over(0, 2, lambda j, a: half(colour, j * (pairs - 1), mode, a), acc)
        if n < 4:
            send_theta(n + 1, colour)
            send_rad(functools.partial(field_copy, n + 1, colour))
        if mode == 1:
            sums[1] = acc
        if mode == 2:
            sums[0] = acc

    part[0] = sums[1] * (1.0 / 9.0) + sums[0] * (1.0 / 2.25)
    for level, peers in enumerate(groups):
        for j, p in enumerate(peers):
            pltpu.make_async_remote_copy(
                part.at[level], gather.at[level, j], ar_send.at[level], ar_recv.at[level], device_id=p, device_id_type=MESH
            ).start()
        if level == 0:
            def unpack(j, _):
                c, k = j // pairs, j % pairs
                for i in range(tile_rows):
                    for q in range(tiles):
                        a, b = field[0, c, k + 1, q, at(i), :], field[1, c, k + 1, q, at(i), :]
                        x, y = jnp.where(even, a, b), jnp.where(even, b, a)
                        n = LANES if q < tiles - 1 else last_lanes
                        raw_d[c, 2 * k, pl.ds(8 * i, 8), pl.ds(q * LANES, n)] = x[:, :n]
                        raw_d[c, 2 * k + 1, pl.ds(8 * i, 8), pl.ds(q * LANES, n)] = y[:, :n]
                return 0

            lax.fori_loop(0, 3 * pairs, unpack, 0)
            pltpu.make_async_copy(raw_d, out_hbm, out_sem.at[0]).start()
        everything = gather.at[level, pl.ds(0, len(peers))]
        pltpu.make_async_copy(everything, everything, ar_recv.at[level]).wait()
        part[level + 1] = part[level] + jnp.sum(gather[level, : len(peers)], axis=0)
    norm_ref[...] = jnp.sqrt(jnp.sum(part[len(groups)], keepdims=True) / count)

    for level, peers in enumerate(groups):
        everything = gather.at[level, pl.ds(0, len(peers))]
        pltpu.make_async_copy(everything, everything, ar_send.at[level]).wait()
    for copy in edge_copies:
        copy.wait_send()
    for colour in range(2):
        drain_rad(functools.partial(stiff_copy, colour))
    for n in range(5):
        for copy in theta_copies(n):
            copy.wait_send()
    drain_rad(functools.partial(field_copy, 4, 1))
    pltpu.make_async_copy(raw_d, out_hbm, out_sem.at[0]).wait()


def make_levels(n_theta, n_rad):
    plane = 8 if n_theta % 8 == 0 else n_theta
    stacks = n_theta // plane

    def within(t, r):
        z, x = t // plane, lax.rem(t, plane)
        return [
            (z * plane + lax.rem(x + i, plane), lax.rem(r + j, n_rad))
            for j in range(n_rad) for i in range(plane) if i or j
        ]

    def across(t, r):
        return [(lax.rem(t + i * plane, n_theta), r) for i in range(1, stacks)]

    return (within, across), (n_rad * plane - 1, stacks - 1)


def solution(mesh):
    n_theta, n_rad = mesh.shape["theta"], mesh.shape["rad"]
    levels, sizes = make_levels(n_theta, n_rad)

    def shards(displacement, stiffness, wall):
        planes, rows, cols = stiffness.shape
        pairs, tiles = planes // 2, -(-cols // LANES)
        count = 3.0 * planes * rows * cols * n_theta * n_rad
        cfg = (n_theta, n_rad, pairs, rows, cols, tiles, levels, count)
        dma = pltpu.SemaphoreType.DMA
        moved, norm = pl.pallas_call(
            functools.partial(kernel, cfg),
            out_shape=(jax.ShapeDtypeStruct(displacement.shape, F32), jax.ShapeDtypeStruct((1, 1), F32)),
            in_specs=[pl.BlockSpec(memory_space=pl.ANY)] * 3,
            out_specs=(pl.BlockSpec(memory_space=pl.ANY), pl.BlockSpec(memory_space=pltpu.VMEM)),
            scratch_shapes=[
                pltpu.VMEM((3, planes, rows, cols), F32),
                pltpu.VMEM((planes, rows, cols), F32),
                pltpu.VMEM((planes, rows, cols), jnp.int32),
                pltpu.VMEM((2, 3, pairs + 2, tiles, rows + 16, LANES), F32),
                pltpu.VMEM((2, pairs + 2, tiles, rows + 16, LANES), F32),
                pltpu.VMEM((2, 7, pairs, tiles, rows, LANES), F32),
                pltpu.VMEM((5, 2, 3, tiles, rows // 2, LANES), F32),
                pltpu.VMEM((5, 2, 3, tiles, rows // 2, LANES), F32),
                pltpu.VMEM((2, rows, cols), F32),
                pltpu.VMEM((3, 8, LANES), F32),
                pltpu.VMEM((2, max(sizes), 8, LANES), F32),
                dma((3,)), dma((1,)), dma((5, 2)), dma((5, 2)), dma((2,)), dma((2,)),
                dma((5, 2)), dma((5, 2)), dma((2, 2)), dma((2, 2)), dma((2,)), dma((2,)),
            ],
            compiler_params=pltpu.CompilerParams(collective_id=0, has_side_effects=True, vmem_limit_bytes=48 * 2**20),
            cost_estimate=pl.CostEstimate(flops=10**8, bytes_accessed=4 * 10**6, transcendentals=0),
        )(displacement, stiffness, wall)
        return moved, norm.reshape(())

    placed = (P(None, "theta", "rad", None), P("theta", "rad", None), P("theta", "rad", None))
    return jax.shard_map(
        shards, mesh=mesh, in_specs=placed, out_specs=(P(None, "theta", "rad", None), P()), check_vma=False,
    )
```

time: 203 us -> 61.9 us (0.30)
  blocking collectives: 77.5 us -> 0 us
  starting transfers between devices: 60.9 us -> 0 us
  Pallas kernels: 0 us -> 54.5 us
  waiting for transfers between devices: 40.3 us -> 0 us
  other arithmetic: 19.1 us -> 0 us
  local copies, waits for them, and re-layouts: 2.48 us -> 4.81 us
    psum x1 -> x0, blocking collectives: 77.5 us -> none  [shards(): squared = lax.psum(jnp.sum(residual * residual), ('theta', 'rad'))]
    ppermute x24 -> x0, starting transfers between devices: 60.9 us -> none  [the longest x12 52.1 us: with_halo(): after = lax.ppermute(initial, axis, down)]
    pallas_call x0 -> x1, Pallas kernels: none -> 54.5 us  [shards(): pl.pallas_call(functools.partial(kernel, cfg), out_shape=(jax.ShapeDtypeS...]
    ppermute x24 -> x0, waiting for transfers between devices: 40.3 us -> none  [the longest x12 25.6 us: with_halo(): before = lax.ppermute(last, axis, up)]
    select_n x11 -> x0, other arithmetic: 12.9 us -> none  [the longest x4 10.2 us: relax(): return (jnp.where(chosen, updated, center), average - center)]
    unnamed x12 -> x7, local copies, waits for them, and re-layouts: 0.21 us -> 4.81 us
    reduce_sum x1 -> x0, other arithmetic: 3.1 us -> none  [shards(): squared = lax.psum(jnp.sum(residual * residual), ('theta', 'rad'))]
    slice x10 -> x0, local copies, waits for them, and re-layouts: 2.26 us -> none  [the longest x2 1.89 us: with_halo(): initial = lax.slice_in_dim(x, 0, width, axis=dim)]
  transfers between devices with their start and end apart: 24 -> 0, of which waited for: 17 -> 0; matrix products, arithmetic and copies ran while one was open for 2% -> 0% of each run, Pallas kernels for 0% -> 0%
where the time goes in v1:
time: 61.9 us; the launch traced here: 61.7 us
  Pallas kernels  54.5 us (88%)
  local copies, waits for them, and re-layouts  4.81 us (8%)
  between operations  2.39 us (4%)
    pallas_call x1, Pallas kernels, shards(): pl.pallas_call(functools.partial(kernel, cfg), out_shape=(jax.ShapeDtypeS...  54.5 us
    unnamed x7, local copies, waits for them, and re-layouts  4.81 us

profile of v1, /device:TPU:1, one launch (start us, length us, event | category | flops | bytes accessed | tf_op | source)
XLA Modules:
  0.0 61.7 jit_solution(8563469979725398679)
XLA Ops:
  0.6 0.0 copy-start
  0.6 1.5 %copy-done = f32[3,12,32,320]{3,2,1,0:T(8,128)S(1)} copy-done((f32[3,12,32,320]{3,2,1,0:T(8,128)S(1)}, f32[3,12,32,320]{3,2,1,0:T(8,128)}, u32[]{:S(2)}) %copy-start) | copy-done | bytes 1474584
  2.1 0.0 copy-start.1
  2.1 1.1 %copy-done.1 = f32[12,32,320]{2,1,0:T(8,128)S(1)} copy-done((f32[12,32,320]{2,1,0:T(8,128)S(1)}, f32[12,32,320]{2,1,0:T(8,128)}, u32[]{:S(2)}) %copy-start.1) | copy-done | bytes 491544
  3.2 0.0 copy-start.2
  3.2 1.1 %copy-done.2 = s32[12,32,320]{2,1,0:T(8,128)S(1)} copy-done((s32[12,32,320]{2,1,0:T(8,128)S(1)}, s32[12,32,320]{2,1,0:T(8,128)}, u32[]{:S(2)}) %copy-start.2) | copy-done | bytes 491544
  4.2 54.5 %shard_map.50 = (f32[3,12,32,320]{3,2,1,0:T(8,128)S(1)}, f32[1,1]{1,0:T(1,128)}) custom-call(f32[3,12,32,320]{3,2,1,0:T(8,128)S(1)} %copy-done, f32[12,32,320]{2,1,0:T(8,128)S(1)} %copy-done.1, s32[12,32,320]{2,1,0:T(8,128)S(1)} %copy-done.2), custom_call_target="tpu_custom_call" | custom-call | flops 100000000 | bytes 4000000 | tf_op jit(solution)/shard_map/pallas_call | solution.py:389
  58.7 1.2 %copy.7 = f32[3,12,32,320]{3,2,1,0:T(8,128)} copy(f32[3,12,32,320]{3,2,1,0:T(8,128)S(1)} %get-tuple-element.8) | data formatting | bytes 2949120
Async XLA Ops:
  0.6 1.5 %copy-start = (f32[3,12,32,320]{3,2,1,0:T(8,128)S(1)}, f32[3,12,32,320]{3,2,1,0:T(8,128)}, u32[]{:S(2)}) copy-start(f32[3,12,32,320]{3,2,1,0:T(8,128)} %d_hbm.1) | copy-start | bytes 4423684
  2.1 1.1 %copy-start.1 = (f32[12,32,320]{2,1,0:T(8,128)S(1)}, f32[12,32,320]{2,1,0:T(8,128)}, u32[]{:S(2)}) copy-start(f32[12,32,320]{2,1,0:T(8,128)} %s_hbm.1) | copy-start | bytes 1474564
  3.2 1.1 %copy-start.2 = (s32[12,32,320]{2,1,0:T(8,128)S(1)}, s32[12,32,320]{2,1,0:T(8,128)}, u32[]{:S(2)}) copy-start(s32[12,32,320]{2,1,0:T(8,128)} %w_hbm.1) | copy-start | bytes 1474564

commit v2 on v1

v2 whole, which is shorter than its diff:
```python
import functools

import jax
import jax.numpy as jnp
from jax import lax
from jax.experimental import pallas as pl
from jax.experimental.pallas import tpu as pltpu
from jax.sharding import PartitionSpec as P

MESH = pl.DeviceIdType.MESH
F32 = jnp.float32
LANES = 128
OFF = 8
SELF, IN, OUT, RP, RM, AP, AM = range(7)


def iota(dim):
    return lax.broadcasted_iota(jnp.int32, (8, LANES), dim)


def kernel(
    cfg, d_hbm, s_hbm, w_hbm, out_hbm, norm_ref,
    raw_d, raw_s, raw_w, field, last, stiff, weight, scale_b, first_out, first_in, stage, land, land_g,
    rad_in, rad_g, corner, edge_s, edge_c, w_theta, w_rad, w_face, w_corner, part, gather,
    load_sem, out_sem, f_send, f_recv, t_send, t_recv, g_send, g_recv, es_send, es_recv, ec_send, ec_recv,
    rs_send, rs_recv, r0_send, r0_recv, rd_send, rd_recv, rg_send, rg_recv, c_send, c_recv, ar_send, ar_recv,
):
    n_theta, n_rad, pairs, rows, cols, tiles, levels, count = cfg
    t, r = lax.axis_index("theta"), lax.axis_index("rad")
    tile_rows = rows // 8
    last_lanes = cols - (tiles - 1) * LANES
    t_next, t_prev = lax.rem(t + 1, n_theta), lax.rem(t + n_theta - 1, n_theta)
    r_up, r_down = lax.rem(r + 1, n_rad), lax.rem(r + n_rad - 1, n_rad)
    beside_t = (t_prev, t_next)
    beside_r = (r_down, r_up)
    has = (r > 0, r < n_rad - 1)
    rim = (1, pairs)
    ghost = (0, pairs + 1)
    edge_row = (OFF, OFF + rows - 1)
    beyond = (OFF - 1, OFF + rows)
    own = pl.ds(1, pairs)

    loads = [
        pltpu.make_async_copy(s_hbm, raw_s, load_sem.at[0]),
        pltpu.make_async_copy(d_hbm, raw_d, load_sem.at[1]),
        pltpu.make_async_copy(w_hbm, raw_w, load_sem.at[2]),
    ]
    for c in loads:
        c.start()

    groups = [level(t, r) for level in levels]
    barrier = pltpu.get_barrier_semaphore()
    diagonal = [(tt, rr) for tt in beside_t for rr in beside_r]
    greet = [(tt, r) for tt in beside_t] + diagonal + [p for g in groups for p in g]
    for p in greet:
        pl.semaphore_signal(barrier, inc=1, device_id=p, device_id_type=MESH)

    even = (iota(0) + iota(1)) % 2 == 0
    odd = jnp.logical_not(even)
    lane = lax.broadcasted_iota(jnp.int32, (1, LANES), 1)
    first_lane, last_lane = iota(1) == 0, iota(1) == LANES - 1
    inside = iota(1) < last_lanes
    at_first_col, at_last_col = iota(1) == 0, iota(1) == last_lanes - 1

    def facing(colour, side):
        return even if colour == side else odd

    def raw_tile(ref, lead, i, q):
        if q < tiles - 1:
            return ref[(*lead, pl.ds(8 * i, 8), pl.ds(q * LANES, LANES))]
        x = ref[(*lead, pl.ds(8 * i, 8), pl.ds(q * LANES, last_lanes))]
        if last_lanes == LANES:
            return x
        return jnp.concatenate([x, jnp.zeros((8, LANES - last_lanes), x.dtype)], axis=1)

    def raw_row(ref, lead, q):
        if q < tiles - 1:
            return ref[(*lead, pl.ds(0, 1), pl.ds(q * LANES, LANES))]
        x = ref[(*lead, pl.ds(0, 1), pl.ds(q * LANES, last_lanes))]
        if last_lanes == LANES:
            return x
        return jnp.concatenate([x, jnp.zeros((1, LANES - last_lanes), x.dtype)], axis=1)

    def at(i, shift=0):
        return pl.ds(OFF + 8 * i + shift, 8)

    def one(row):
        return pl.ds(row, 1)

    zero_row = jnp.zeros((1, LANES), F32)
    zero = jnp.zeros((8, LANES), F32)
    loads[0].wait()

    def pack_s(k, _):
        for i in range(tile_rows):
            for q in range(tiles):
                a, b = raw_tile(raw_s, (2 * k,), i, q), raw_tile(raw_s, (2 * k + 1,), i, q)
                stiff[0, k + 1, q, at(i), :] = jnp.where(even, a, b)
                stiff[1, k + 1, q, at(i), :] = jnp.where(even, b, a)
        return 0

    lax.fori_loop(0, pairs, pack_s, 0)
    loads[1].wait()

    def pack_d(j, _):
        c, k = j // pairs, j % pairs
        for i in range(tile_rows):
            for q in range(tiles):
                a, b = raw_tile(raw_d, (c, 2 * k), i, q), raw_tile(raw_d, (c, 2 * k + 1), i, q)
                field[0, c, k + 1, q, at(i), :] = jnp.where(even, a, b)
                field[1, c, k + 1, q, at(i), :] = jnp.where(even, b, a)
        for q in range(tiles):
            for row in beyond:
                field[0, c, k + 1, q, one(row), :] = zero_row
                last[c, k + 1, q, one(row), :] = zero_row
        return 0

    lax.fori_loop(0, 3 * pairs, pack_d, 0)
    for end in range(2):
        @pl.when(jnp.logical_not(has[end]))
        def _():
            def clear(k, _):
                for q in range(tiles):
                    stiff[0, k + 1, q, one(beyond[end]), :] = zero_row
                    stiff[1, k + 1, q, one(beyond[end]), :] = zero_row
                    for c in range(3):
                        field[1, c, k + 1, q, one(beyond[end]), :] = zero_row
                return 0

            lax.fori_loop(0, pairs, clear, 0)

    for c in range(3):
        for g in ghost:
            for q in range(tiles):
                for i in range(tile_rows):
                    field[0, c, g, q, at(i), :] = zero
    loads[2].wait()

    def to(tt, rr):
        return {"device_id": (tt, rr), "device_id_type": MESH}

    def remote(src, dst, send, recv, where):
        return pltpu.make_async_remote_copy(src, dst, send, recv, **where)

    edge_copies = [
        remote(raw_s.at[0 if side == 0 else 2 * pairs - 1], edge_s.at[1 - side], es_send.at[side], es_recv.at[1 - side], to(beside_t[side], r))
        for side in range(2)
    ]
    first_copies = [
        remote(first_out.at[side], first_in.at[1 - side], f_send.at[side], f_recv.at[1 - side], to(beside_t[side], r))
        for side in range(2)
    ]

    def theta_copies(n):
        return [
            remote(stage.at[n, side], land.at[n, 1 - side], t_send.at[n, side], t_recv.at[n, 1 - side], to(beside_t[side], r))
            for side in range(2)
        ]

    g_copies = [
        remote(scale_b.at[rim[side] - 1], land_g.at[1 - side], g_send.at[side], g_recv.at[1 - side], to(beside_t[side], r))
        for side in range(2)
    ]

    def stiff_rows(end):
        return [
            remote(
                stiff.at[colour, own, slice(None), one(edge_row[end])], stiff.at[colour, own, slice(None), one(beyond[1 - end])],
                rs_send.at[colour, end], rs_recv.at[colour, 1 - end], to(t, beside_r[end]),
            )
            for colour in range(2)
        ]

    def edge_corners(end):
        return [
            remote(
                raw_s.at[0 if side == 0 else 2 * pairs - 1, pl.ds(0 if end == 0 else rows - 1, 1)], edge_c.at[1 - side, 1 - end],
                ec_send.at[side, end], ec_recv.at[1 - side, 1 - end], to(beside_t[side], beside_r[end]),
            )
            for side in range(2)
        ]

    def first_rows(end):
        return [
            remote(
                field.at[1, slice(None), own, slice(None), one(edge_row[end])], field.at[1, slice(None), own, slice(None), one(beyond[1 - end])],
                r0_send.at[end], r0_recv.at[1 - end], to(t, beside_r[end]),
            )
        ]

    def black(n):
        return field.at[1] if n == 0 else last

    def both_rows(n, end):
        return [
            remote(
                ref.at[slice(None), own, slice(None), one(edge_row[end])], rad_in.at[n, colour, 1 - end],
                rd_send.at[n, colour, end], rd_recv.at[n, colour, 1 - end], to(t, beside_r[end]),
            )
            for colour, ref in ((0, field.at[0]), (1, black(n)))
        ]

    def scale_rows(end):
        return [
            remote(
                scale_b.at[slice(None), slice(None), one(edge_row[end] - OFF)], rad_g.at[1 - end],
                rg_send.at[end], rg_recv.at[1 - end], to(t, beside_r[end]),
            )
        ]

    def red_corners(n, end):
        return [
            remote(
                field.at[0, slice(None), rim[side], slice(None), one(edge_row[end])], corner.at[n, 1 - side, 1 - end],
                c_send.at[n, side, end], c_recv.at[n, 1 - side, 1 - end], to(beside_t[side], beside_r[end]),
            )
            for side in range(2)
        ]

    def by_end(copies, what):
        for end in range(2):
            @pl.when(has[end])
            def _():
                for copy in copies(end if what != "take" else 1 - end):
                    if what == "start":
                        copy.start()
                    elif what == "take":
                        copy.wait_recv()
                    else:
                        copy.wait_send()

    def send_first():
        for side in range(2):
            keep = facing(1, side)
            for c in range(3):
                for q in range(tiles):
                    for h in range(tile_rows // 2):
                        a = field[1, c, rim[side], q, at(2 * h), :]
                        b = field[1, c, rim[side], q, at(2 * h + 1), :]
                        first_out[side, c, q, pl.ds(8 * h, 8), :] = jnp.where(keep, a, pltpu.roll(b, 1, 0))
        for copy in first_copies:
            copy.start()

    def take_first():
        for copy in first_copies:
            copy.wait_recv()
        for side in range(2):
            for c in range(3):
                for q in range(tiles):
                    for h in range(tile_rows // 2):
                        x = first_in[side, c, q, pl.ds(8 * h, 8), :]
                        field[1, c, ghost[side], q, at(2 * h), :] = x
                        field[1, c, ghost[side], q, at(2 * h + 1), :] = pltpu.roll(x, 7, 0)

    def send_theta(n):
        for side in range(2):
            red_here = facing(0, side)
            for c in range(3):
                for q in range(tiles):
                    for i in range(tile_rows):
                        x = field[0, c, rim[side], q, at(i), :]
                        y = black(n)[c, rim[side], q, at(i), :]
                        stage[n, side, c, q, pl.ds(8 * i, 8), :] = jnp.where(red_here, x, y)
        for copy in theta_copies(n):
            copy.start()
        by_end(functools.partial(red_corners, n), "start")

    pl.semaphore_wait(barrier, len(greet))
    for copy in edge_copies:
        copy.start()
    send_first()
    by_end(stiff_rows, "start")
    by_end(first_rows, "start")
    by_end(edge_corners, "start")

    def beside(v, side):
        out = []
        for q in range(tiles):
            if side:
                x = pltpu.roll(v[q], LANES - 1, 1)
                if q < tiles - 1:
                    x = jnp.where(last_lane, pltpu.roll(v[q + 1], LANES - 1, 1), x)
            else:
                x = pltpu.roll(v[q], 1, 1)
                if q > 0:
                    x = jnp.where(first_lane, pltpu.roll(v[q - 1], 1, 1), x)
            out.append(x)
        return out

    def outer(colour, before, after):
        return jnp.where(even, before, after) if colour == 0 else jnp.where(even, after, before)

    def make_weights(colour, k):
        other = 1 - colour
        for i in range(tile_rows):
            mid = [stiff[other, k + 1, q, at(i), :] for q in range(tiles)]
            forth, back = beside(mid, 1), beside(mid, 0)
            for q in range(tiles):
                s = stiff[colour, k + 1, q, at(i), :]
                faces = [None] * 7
                faces[IN] = s + mid[q]
                faces[OUT] = s + outer(colour, stiff[other, k, q, at(i), :], stiff[other, k + 2, q, at(i), :])
                faces[RP] = s + stiff[other, k + 1, q, at(i, 1), :]
                faces[RM] = s + stiff[other, k + 1, q, at(i, -1), :]
                ap, am = forth[q], back[q]
                if q == tiles - 1:
                    ap = jnp.where(at_last_col, s, ap)
                if q == 0:
                    am = jnp.where(at_first_col, s, am)
                faces[AP], faces[AM] = s + ap, s + am
                total = faces[IN] + faces[OUT] + (faces[RP] + faces[RM]) + (faces[AP] + faces[AM])
                wa, wb = raw_tile(raw_w, (2 * k,), i, q), raw_tile(raw_w, (2 * k + 1,), i, q)
                fixed = (jnp.where(even, wa, wb) if colour == 0 else jnp.where(even, wb, wa)) != 0
                if q == tiles - 1 and last_lanes < LANES:
                    fixed = jnp.logical_or(fixed, jnp.logical_not(inside))
                scale = jnp.where(fixed, 0.0, 1.5 / total)
                put = pl.ds(8 * i, 8)
                if colour == 1:
                    scale_b[k, q, put, :] = scale
                weight[colour, SELF, k, q, put, :] = jnp.where(fixed, 1.0, -0.5)
                for f in (IN, OUT, RP, RM, AP, AM):
                    w = faces[f] * scale
                    if f == AP and q == tiles - 1:
                        w = jnp.where(at_last_col, 0.0, w)
                    if f == AM and q == 0:
                        w = jnp.where(at_first_col, 0.0, w)
                    weight[colour, f, k, q, put, :] = w

    def half(colour, k, opp, cur, dst, acc=None):
        for i in range(tile_rows):
            put = pl.ds(8 * i, 8)
            w = [[weight[colour, f, k, q, put, :] for q in range(tiles)] for f in range(7)]
            for c in range(3):
                mid = [opp[c, k + 1, q, at(i), :] for q in range(tiles)]
                forth, back = beside(mid, 1), beside(mid, 0)
                for q in range(tiles):
                    far = outer(colour, opp[c, k, q, at(i), :], opp[c, k + 2, q, at(i), :])
                    old = cur[c, k + 1, q, at(i), :]
                    new = w[SELF][q] * old + w[IN][q] * mid[q] + w[OUT][q] * far
                    new = new + w[RP][q] * opp[c, k + 1, q, at(i, 1), :]
                    new = new + w[RM][q] * opp[c, k + 1, q, at(i, -1), :]
                    new = new + w[AP][q] * forth[q] + w[AM][q] * back[q]
                    if dst is not None:
                        dst[c, k + 1, q, at(i), :] = new
                    if acc is not None:
                        change = new - old
                        acc = acc + change * change
        return acc

    def inner(fn):
        lax.fori_loop(1, pairs - 1, lambda k, _: (fn(k), 0)[1], 0)

    def rims(fn):
        lax.fori_loop(0, 2, lambda j, _: (fn(j * (pairs - 1)), 0)[1], 0)

    def face_weights():
        for side in range(2):
            k = rim[side]
            for q in range(tiles):
                for i in range(tile_rows):
                    put = pl.ds(8 * i, 8)
                    w_theta[side, q, put, :] = (stiff[1, ghost[side], q, at(i), :] + stiff[0, k, q, at(i), :]) * land_g[side, q, put, :]
        for end in range(2):
            @pl.when(has[end])
            def _():
                for q in range(tiles):
                    for side in range(2):
                        s = stiff[1, ghost[side], q, one(edge_row[end]), :]
                        g = land_g[side, q, one(edge_row[end] - OFF), :]
                        x = raw_row(edge_c, (side, end), q)
                        w_corner[side, end, q] = (s + x) * g
                        k = rim[side]
                        parity = (beyond[end] + lane) % 2 == 0
                        here = parity if side == 1 else jnp.logical_not(parity)
                        w_face[side, end, q] = jnp.where(here, (stiff[1, k, q, one(beyond[end]), :] + x) * rad_g[end, k - 1, q], 0.0)

    def rad_weights():
        for end in range(2):
            @pl.when(has[end])
            def _():
                def body(k, _):
                    for q in range(tiles):
                        w_rad[end, k, q] = (stiff[1, k + 1, q, one(beyond[end]), :] + stiff[0, k + 1, q, one(edge_row[end]), :]) * rad_g[end, k, q]
                    return 0

                lax.fori_loop(0, pairs, body, 0)

    def cross_rad(n):
        dst = black(n)
        for end in range(2):
            @pl.when(has[end])
            def _():
                f = RP if end else RM

                def body(k, _):
                    for q in range(tiles):
                        w = weight[1, f, k, q, one(edge_row[end] - OFF), :]
                        wg = w_rad[end, k, q]
                        for c in range(3):
                            here = (c, k + 1, q, one(edge_row[end]), slice(None))
                            dst[here] = dst[here] + w * rad_in[n, 0, end, c, k, q]
                            dst[c, k + 1, q, one(beyond[end]), :] = rad_in[n, 1, end, c, k, q] + wg * field[(0, *here)]
                    return 0

                lax.fori_loop(0, pairs, body, 0)

    def cross_theta(n):
        dst = black(n)
        for side in range(2):
            k, here = rim[side], facing(1, side)
            for q in range(tiles):
                for i in range(tile_rows):
                    put = pl.ds(8 * i, 8)
                    w = jnp.where(here, weight[1, OUT, k - 1, q, put, :], 0.0)
                    wg = w_theta[side, q, put, :]
                    for c in range(3):
                        x = land[n, side, c, q, put, :]
                        dst[c, k, q, at(i), :] = dst[c, k, q, at(i), :] + w * x
                        dst[c, ghost[side], q, at(i), :] = x + wg * field[0, c, k, q, at(i), :]
        for end in range(2):
            @pl.when(has[end])
            def _():
                for side in range(2):
                    k = rim[side]
                    for q in range(tiles):
                        for c in range(3):
                            x = corner[n, side, end, c, q]
                            a = (c, ghost[side], q, one(edge_row[end]), slice(None))
                            b = (c, k, q, one(beyond[end]), slice(None))
                            dst[a] = dst[a] + w_corner[side, end, q] * x
                            dst[b] = dst[b] + w_face[side, end, q] * x

    red, black0 = field.at[0], field.at[1]

    by_end(stiff_rows, "take")
    inner(lambda k: (make_weights(0, k), make_weights(1, k)))
    by_end(first_rows, "take")
    inner(lambda k: half(0, k, black0, red, red))
    for copy in edge_copies:
        copy.wait_recv()
    for side in range(2):
        for i in range(tile_rows):
            for q in range(tiles):
                x = raw_tile(edge_s, (side,), i, q)
                stiff[0, ghost[side], q, at(i), :] = x
                stiff[1, ghost[side], q, at(i), :] = x
    rims(lambda k: (make_weights(0, k), make_weights(1, k)))
    for copy in g_copies:
        copy.start()
    by_end(scale_rows, "start")
    take_first()
    rims(lambda k: half(0, k, black0, red, red))
    by_end(first_rows, "drain")
    rims(lambda k: half(1, k, red, black0, black0))
    send_theta(0)
    inner(lambda k: half(1, k, red, black0, black0))
    by_end(functools.partial(both_rows, 0), "start")

    by_end(scale_rows, "take")
    rad_weights()
    by_end(functools.partial(both_rows, 0), "take")
    by_end(functools.partial(both_rows, 0), "drain")
    cross_rad(0)
    by_end(functools.partial(red_corners, 0), "drain")
    inner(lambda k: half(0, k, black0, red, red))
    for copy in g_copies:
        copy.wait_recv()
    by_end(edge_corners, "take")
    face_weights()
    for copy in theta_copies(0):
        copy.wait_recv()
    by_end(functools.partial(red_corners, 0), "take")
    cross_theta(0)
    rims(lambda k: half(0, k, black0, red, red))
    rims(lambda k: half(1, k, red, black0, last))
    send_theta(1)
    inner(lambda k: half(1, k, red, black0, last))
    by_end(functools.partial(both_rows, 1), "start")

    def squares(k, acc):
        for i in range(tile_rows):
            for q in range(tiles):
                for c in range(3):
                    change = last[c, k + 1, q, at(i), :] - field[1, c, k + 1, q, at(i), :]
                    acc = acc + change * change
        return acc

    by_end(functools.partial(both_rows, 1), "take")
    by_end(functools.partial(both_rows, 1), "drain")
    cross_rad(1)
    red_sum = lax.fori_loop(1, pairs - 1, lambda k, a: half(0, k, last, red, None, a), zero)
    black_sum = lax.fori_loop(1, pairs - 1, squares, zero)
    for copy in theta_copies(1):
        copy.wait_recv()
    by_end(functools.partial(red_corners, 1), "take")
    cross_theta(1)
    red_sum = lax.fori_loop(0, 2, lambda j, a: half(0, j * (pairs - 1), last, red, None, a), red_sum)
    black_sum = lax.fori_loop(0, 2, lambda j, a: squares(j * (pairs - 1), a), black_sum)

    part[0] = black_sum * (1.0 / 9.0) + red_sum * (1.0 / 2.25)
    for level, peers in enumerate(groups):
        for j, p in enumerate(peers):
            pltpu.make_async_remote_copy(
                part.at[level], gather.at[level, j], ar_send.at[level], ar_recv.at[level], device_id=p, device_id_type=MESH
            ).start()
        if level == 0:
            def unpack(j, _):
                c, k = j // pairs, j % pairs
                for i in range(tile_rows):
                    for q in range(tiles):
                        a, b = field[0, c, k + 1, q, at(i), :], last[c, k + 1, q, at(i), :]
                        x, y = jnp.where(even, a, b), jnp.where(even, b, a)
                        n = LANES if q < tiles - 1 else last_lanes
                        raw_d[c, 2 * k, pl.ds(8 * i, 8), pl.ds(q * LANES, n)] = x[:, :n]
                        raw_d[c, 2 * k + 1, pl.ds(8 * i, 8), pl.ds(q * LANES, n)] = y[:, :n]
                return 0

            lax.fori_loop(0, 3 * pairs, unpack, 0)
            pltpu.make_async_copy(raw_d, out_hbm, out_sem.at[0]).start()
        everything = gather.at[level, pl.ds(0, len(peers))]
        pltpu.make_async_copy(everything, everything, ar_recv.at[level]).wait()
        part[level + 1] = part[level] + jnp.sum(gather[level, : len(peers)], axis=0)
    norm_ref[...] = jnp.sqrt(jnp.sum(part[len(groups)], keepdims=True) / count)

    for level, peers in enumerate(groups):
        everything = gather.at[level, pl.ds(0, len(peers))]
        pltpu.make_async_copy(everything, everything, ar_send.at[level]).wait()
    for copy in edge_copies + first_copies + g_copies + theta_copies(0) + theta_copies(1):
        copy.wait_send()
    for copies in (stiff_rows, edge_corners, scale_rows, functools.partial(red_corners, 1)):
        by_end(copies, "drain")
    pltpu.make_async_copy(raw_d, out_hbm, out_sem.at[0]).wait()


def make_levels(n_theta, n_rad):
    plane = 8 if n_theta % 8 == 0 else n_theta
    stacks = n_theta // plane

    def within(t, r):
        z, x = t // plane, lax.rem(t, plane)
        return [
            (z * plane + lax.rem(x + i, plane), lax.rem(r + j, n_rad))
            for j in range(n_rad) for i in range(plane) if i or j
        ]

    def across(t, r):
        return [(lax.rem(t + i * plane, n_theta), r) for i in range(1, stacks)]

    return (within, across), (n_rad * plane - 1, stacks - 1)


def solution(mesh):
    n_theta, n_rad = mesh.shape["theta"], mesh.shape["rad"]
    levels, sizes = make_levels(n_theta, n_rad)

    def shards(displacement, stiffness, wall):
        planes, rows, cols = stiffness.shape
        pairs, tiles = planes // 2, -(-cols // LANES)
        count = 3.0 * planes * rows * cols * n_theta * n_rad
        cfg = (n_theta, n_rad, pairs, rows, cols, tiles, levels, count)
        dma = pltpu.SemaphoreType.DMA
        moved, norm = pl.pallas_call(
            functools.partial(kernel, cfg),
            out_shape=(jax.ShapeDtypeStruct(displacement.shape, F32), jax.ShapeDtypeStruct((1, 1), F32)),
            in_specs=[pl.BlockSpec(memory_space=pl.ANY)] * 3,
            out_specs=(pl.BlockSpec(memory_space=pl.ANY), pl.BlockSpec(memory_space=pltpu.VMEM)),
            scratch_shapes=[
                pltpu.VMEM((3, planes, rows, cols), F32),
                pltpu.VMEM((planes, rows, cols), F32),
                pltpu.VMEM((planes, rows, cols), jnp.int32),
                pltpu.VMEM((2, 3, pairs + 2, tiles, rows + 16, LANES), F32),
                pltpu.VMEM((3, pairs + 2, tiles, rows + 16, LANES), F32),
                pltpu.VMEM((2, pairs + 2, tiles, rows + 16, LANES), F32),
                pltpu.VMEM((2, 7, pairs, tiles, rows, LANES), F32),
                pltpu.VMEM((pairs, tiles, rows, LANES), F32),
                pltpu.VMEM((2, 3, tiles, rows // 2, LANES), F32),
                pltpu.VMEM((2, 3, tiles, rows // 2, LANES), F32),
                pltpu.VMEM((2, 2, 3, tiles, rows, LANES), F32),
                pltpu.VMEM((2, 2, 3, tiles, rows, LANES), F32),
                pltpu.VMEM((2, tiles, rows, LANES), F32),
                pltpu.VMEM((2, 2, 2, 3, pairs, tiles, 1, LANES), F32),
                pltpu.VMEM((2, pairs, tiles, 1, LANES), F32),
                pltpu.VMEM((2, 2, 2, 3, tiles, 1, LANES), F32),
                pltpu.VMEM((2, rows, cols), F32),
                pltpu.VMEM((2, 2, 1, cols), F32),
                pltpu.VMEM((2, tiles, rows, LANES), F32),
                pltpu.VMEM((2, pairs, tiles, 1, LANES), F32),
                pltpu.VMEM((2, 2, tiles, 1, LANES), F32),
                pltpu.VMEM((2, 2, tiles, 1, LANES), F32),
                pltpu.VMEM((3, 8, LANES), F32),
                pltpu.VMEM((2, max(sizes), 8, LANES), F32),
                dma((3,)), dma((1,)), dma((2,)), dma((2,)), dma((2, 2)), dma((2, 2)), dma((2,)), dma((2,)),
                dma((2,)), dma((2,)), dma((2, 2)), dma((2, 2)), dma((2, 2)), dma((2, 2)), dma((2,)), dma((2,)),
                dma((2, 2, 2)), dma((2, 2, 2)), dma((2,)), dma((2,)), dma((2, 2, 2)), dma((2, 2, 2)), dma((2,)), dma((2,)),
            ],
            compiler_params=pltpu.CompilerParams(collective_id=0, has_side_effects=True, vmem_limit_bytes=60 * 2**20),
            cost_estimate=pl.CostEstimate(flops=10**8, bytes_accessed=4 * 10**6, transcendentals=0),
        )(displacement, stiffness, wall)
        return moved, norm.reshape(())

    placed = (P(None, "theta", "rad", None), P("theta", "rad", None), P("theta", "rad", None))
    return jax.shard_map(
        shards, mesh=mesh, in_specs=placed, out_specs=(P(None, "theta", "rad", None), P()), check_vma=False,
    )
```

time: 61.9 us -> 51.8 us (0.84)
  Pallas kernels: 54.5 us -> 46.5 us
  local copies, waits for them, and re-layouts: 4.81 us -> 2.8 us
    pallas_call x1, Pallas kernels: 54.5 us -> 46.5 us  [shards(): pl.pallas_call(functools.partial(kernel, cfg), out_shape=(jax.ShapeDtypeS...]
    unnamed x7 -> x1, local copies, waits for them, and re-layouts: 4.81 us -> 2.8 us
where the time goes in v2:
time: 51.8 us; the launch traced here: 51.6 us
  Pallas kernels  46.5 us (90%)
  local copies, waits for them, and re-layouts  2.8 us (5%)
  between operations  2.38 us (5%)
    pallas_call x1, Pallas kernels, shards(): pl.pallas_call(functools.partial(kernel, cfg), out_shape=(jax.ShapeDtypeS...  46.5 us
    unnamed x1, local copies, waits for them, and re-layouts  2.8 us

profile of v2, /device:TPU:1, one launch (start us, length us, event | category | flops | bytes accessed | tf_op | source)
XLA Modules:
  0.0 51.6 jit_solution(861894701106028990)
XLA Ops:
  0.6 46.5 %shard_map.50 = (f32[3,12,32,320]{3,2,1,0:T(8,128)}, f32[1,1]{1,0:T(1,128)}) custom-call(f32[3,12,32,320]{3,2,1,0:T(8,128)} %d_hbm.1, f32[12,32,320]{2,1,0:T(8,128)} %s_hbm.1, s32[12,32,320]{2,1,0:T(8,128)} %w_hbm.1), custom_call_target="tpu_custom_call" | custom-call | flops 100000000 | bytes 4000000 | tf_op jit(solution)/shard_map/pallas_call | solution.py:562
  47.1 2.8 %copy.7 = f32[3,12,32,320]{3,2,1,0:T(8,128)} copy(f32[3,12,32,320]{3,2,1,0:T(8,128)} %get-tuple-element.8) | data formatting | bytes 2949120

commit v3 on v2

--- a/solution.py
+++ b/solution.py
@@ -229,15 +229,42 @@
                     else:
                         copy.wait_send()
 
+    wide, half_lanes = tiles - 1, LANES // 2
+    low = iota(1) < half_lanes
+
+    def put_folded(put, get, n):
+        for c in range(3):
+            for q in range(wide):
+                for i in range(n):
+                    put((c * wide + q) * n + i, get(c, q, i))
+        for i in range(n):
+            put(3 * wide * n + i, jnp.where(low, get(0, wide, i), pltpu.roll(get(1, wide, i), half_lanes, 1)))
+        for i in range(n // 2):
+            x = pltpu.roll(get(2, wide, i + n // 2), half_lanes, 1)
+            put(3 * wide * n + n + i, jnp.where(low, get(2, wide, i), x))
+
+    def get_folded(load, n, c, q, i):
+        if q < wide:
+            return load((c * wide + q) * n + i)
+        if c < 2:
+            x = load(3 * wide * n + i)
+            return pltpu.roll(x, half_lanes, 1) if c else x
+        x = load(3 * wide * n + n + i % (n // 2))
+        return x if i < n // 2 else pltpu.roll(x, half_lanes, 1)
+
     def send_first():
         for side in range(2):
             keep = facing(1, side)
-            for c in range(3):
-                for q in range(tiles):
-                    for h in range(tile_rows // 2):
-                        a = field[1, c, rim[side], q, at(2 * h), :]
-                        b = field[1, c, rim[side], q, at(2 * h + 1), :]
-                        first_out[side, c, q, pl.ds(8 * h, 8), :] = jnp.where(keep, a, pltpu.roll(b, 1, 0))
+
+            def get(c, q, h):
+                a = field[1, c, rim[side], q, at(2 * h), :]
+                b = field[1, c, rim[side], q, at(2 * h + 1), :]
+                return jnp.where(keep, a, pltpu.roll(b, 1, 0))
+
+            def put(j, x):
+                first_out[side, pl.ds(8 * j, 8), :] = x
+
+            put_folded(put, get, tile_rows // 2)
         for copy in first_copies:
             copy.start()
 
@@ -248,30 +275,33 @@
             for c in range(3):
                 for q in range(tiles):
                     for h in range(tile_rows // 2):
-                        x = first_in[side, c, q, pl.ds(8 * h, 8), :]
+                        x = get_folded(lambda j: first_in[side, pl.ds(8 * j, 8), :], tile_rows // 2, c, q, h)
                         field[1, c, ghost[side], q, at(2 * h), :] = x
                         field[1, c, ghost[side], q, at(2 * h + 1), :] = pltpu.roll(x, 7, 0)
 
     def send_theta(n):
         for side in range(2):
             red_here = facing(0, side)
-            for c in range(3):
-                for q in range(tiles):
-                    for i in range(tile_rows):
-                        x = field[0, c, rim[side], q, at(i), :]
-                        y = black(n)[c, rim[side], q, at(i), :]
-                        stage[n, side, c, q, pl.ds(8 * i, 8), :] = jnp.where(red_here, x, y)
+
+            def get(c, q, i):
+                x = field[0, c, rim[side], q, at(i), :]
+                y = black(n)[c, rim[side], q, at(i), :]
+                return jnp.where(red_here, x, y)
+
+            def put(j, x):
+                stage[n, side, pl.ds(8 * j, 8), :] = x
+
+            put_folded(put, get, tile_rows)
         for copy in theta_copies(n):
             copy.start()
-        by_end(functools.partial(red_corners, n), "start")
 
     pl.semaphore_wait(barrier, len(greet))
+    by_end(edge_corners, "start")
     for copy in edge_copies:
         copy.start()
     send_first()
     by_end(stiff_rows, "start")
     by_end(first_rows, "start")
-    by_end(edge_corners, "start")
 
     def beside(v, side):
         out = []
@@ -414,7 +444,7 @@
                     w = jnp.where(here, weight[1, OUT, k - 1, q, put, :], 0.0)
                     wg = w_theta[side, q, put, :]
                     for c in range(3):
-                        x = land[n, side, c, q, put, :]
+                        x = get_folded(lambda j: land[n, side, pl.ds(8 * j, 8), :], tile_rows, c, q, i)
                         dst[c, k, q, at(i), :] = dst[c, k, q, at(i), :] + w * x
                         dst[c, ghost[side], q, at(i), :] = x + wg * field[0, c, k, q, at(i), :]
         for end in range(2):
@@ -450,6 +480,7 @@
     by_end(scale_rows, "start")
     take_first()
     rims(lambda k: half(0, k, black0, red, red))
+    by_end(functools.partial(red_corners, 0), "start")
     by_end(first_rows, "drain")
     rims(lambda k: half(1, k, red, black0, black0))
     send_theta(0)
@@ -472,6 +503,7 @@
     by_end(functools.partial(red_corners, 0), "take")
     cross_theta(0)
     rims(lambda k: half(0, k, black0, red, red))
+    by_end(functools.partial(red_corners, 1), "start")
     rims(lambda k: half(1, k, red, black0, last))
     send_theta(1)
     inner(lambda k: half(1, k, red, black0, last))
@@ -497,11 +529,11 @@
     red_sum = lax.fori_loop(0, 2, lambda j, a: half(0, j * (pairs - 1), last, red, None, a), red_sum)
     black_sum = lax.fori_loop(0, 2, lambda j, a: squares(j * (pairs - 1), a), black_sum)
 
-    part[0] = black_sum * (1.0 / 9.0) + red_sum * (1.0 / 2.25)
+    part[0] = jnp.sum(black_sum * (1.0 / 9.0) + red_sum * (1.0 / 2.25), axis=0, keepdims=True)
     for level, peers in enumerate(groups):
         for j, p in enumerate(peers):
             pltpu.make_async_remote_copy(
-                part.at[level], gather.at[level, j], ar_send.at[level], ar_recv.at[level], device_id=p, device_id_type=MESH
+                part.at[level], gather.at[level, pl.ds(j, 1)], ar_send.at[level], ar_recv.at[level], device_id=p, device_id_type=MESH
             ).start()
         if level == 0:
             def unpack(j, _):
@@ -519,7 +551,7 @@
             pltpu.make_async_copy(raw_d, out_hbm, out_sem.at[0]).start()
         everything = gather.at[level, pl.ds(0, len(peers))]
         pltpu.make_async_copy(everything, everything, ar_recv.at[level]).wait()
-        part[level + 1] = part[level] + jnp.sum(gather[level, : len(peers)], axis=0)
+        part[level + 1] = part[level] + jnp.sum(gather[level, : len(peers)], axis=0, keepdims=True)
     norm_ref[...] = jnp.sqrt(jnp.sum(part[len(groups)], keepdims=True) / count)
 
     for level, peers in enumerate(groups):
@@ -556,12 +588,13 @@
     def shards(displacement, stiffness, wall):
         planes, rows, cols = stiffness.shape
         pairs, tiles = planes // 2, -(-cols // LANES)
+        folded = 3 * (tiles - 1) * rows + rows + rows // 2
         count = 3.0 * planes * rows * cols * n_theta * n_rad
         cfg = (n_theta, n_rad, pairs, rows, cols, tiles, levels, count)
         dma = pltpu.SemaphoreType.DMA
         moved, norm = pl.pallas_call(
             functools.partial(kernel, cfg),
-            out_shape=(jax.ShapeDtypeStruct(displacement.shape, F32), jax.ShapeDtypeStruct((1, 1), F32)),
+            out_shape=(pltpu.VMEM(displacement.shape, F32), jax.ShapeDtypeStruct((1, 1), F32)),
             in_specs=[pl.BlockSpec(memory_space=pl.ANY)] * 3,
             out_specs=(pl.BlockSpec(memory_space=pl.ANY), pl.BlockSpec(memory_space=pltpu.VMEM)),
             scratch_shapes=[
@@ -573,10 +606,10 @@
                 pltpu.VMEM((2, pairs + 2, tiles, rows + 16, LANES), F32),
                 pltpu.VMEM((2, 7, pairs, tiles, rows, LANES), F32),
                 pltpu.VMEM((pairs, tiles, rows, LANES), F32),
-                pltpu.VMEM((2, 3, tiles, rows // 2, LANES), F32),
-                pltpu.VMEM((2, 3, tiles, rows // 2, LANES), F32),
-                pltpu.VMEM((2, 2, 3, tiles, rows, LANES), F32),
-                pltpu.VMEM((2, 2, 3, tiles, rows, LANES), F32),
+                pltpu.VMEM((2, folded // 2, LANES), F32),
+                pltpu.VMEM((2, folded // 2, LANES), F32),
+                pltpu.VMEM((2, 2, folded, LANES), F32),
+                pltpu.VMEM((2, 2, folded, LANES), F32),
                 pltpu.VMEM((2, tiles, rows, LANES), F32),
                 pltpu.VMEM((2, 2, 2, 3, pairs, tiles, 1, LANES), F32),
                 pltpu.VMEM((2, pairs, tiles, 1, LANES), F32),
@@ -587,13 +620,13 @@
                 pltpu.VMEM((2, pairs, tiles, 1, LANES), F32),
                 pltpu.VMEM((2, 2, tiles, 1, LANES), F32),
                 pltpu.VMEM((2, 2, tiles, 1, LANES), F32),
-                pltpu.VMEM((3, 8, LANES), F32),
-                pltpu.VMEM((2, max(sizes), 8, LANES), F32),
+                pltpu.VMEM((3, 1, LANES), F32),
+                pltpu.VMEM((2, -(-max(sizes) // 8) * 8, LANES), F32),
                 dma((3,)), dma((1,)), dma((2,)), dma((2,)), dma((2, 2)), dma((2, 2)), dma((2,)), dma((2,)),
                 dma((2,)), dma((2,)), dma((2, 2)), dma((2, 2)), dma((2, 2)), dma((2, 2)), dma((2,)), dma((2,)),
                 dma((2, 2, 2)), dma((2, 2, 2)), dma((2,)), dma((2,)), dma((2, 2, 2)), dma((2, 2, 2)), dma((2,)), dma((2,)),
             ],
-            compiler_params=pltpu.CompilerParams(collective_id=0, has_side_effects=True, vmem_limit_bytes=60 * 2**20),
+            compiler_params=pltpu.CompilerParams(collective_id=0, has_side_effects=True, vmem_limit_bytes=56 * 2**20),
             cost_estimate=pl.CostEstimate(flops=10**8, bytes_accessed=4 * 10**6, transcendentals=0),
         )(displacement, stiffness, wall)
         return moved, norm.reshape(())

time: 51.8 us -> 47.3 us (0.913)
  Pallas kernels: 46.5 us -> 43.6 us
  local copies, waits for them, and re-layouts: 2.8 us -> 1.21 us
    pallas_call x1, Pallas kernels: 46.5 us -> 43.6 us  [shards(): pl.pallas_call(functools.partial(kernel, cfg), out_shape=(pltpu.VMEM(disp...]
    unnamed x1, local copies, waits for them, and re-layouts: 2.8 us -> 1.21 us
where the time goes in v3:
time: 47.3 us; the launch traced here: 47.2 us
  Pallas kernels  43.6 us (92%)
  between operations  2.33 us (5%)
  local copies, waits for them, and re-layouts  1.21 us (3%)
    pallas_call x1, Pallas kernels, shards(): pl.pallas_call(functools.partial(kernel, cfg), out_shape=(pltpu.VMEM(disp...  43.6 us
    unnamed x1, local copies, waits for them, and re-layouts  1.21 us

profile of v3, /device:TPU:1, one launch (start us, length us, event | category | flops | bytes accessed | tf_op | source)
XLA Modules:
  0.0 47.2 jit_solution(14107991021301618324)
XLA Ops:
  0.6 43.6 %shard_map.50 = (f32[3,12,32,320]{3,2,1,0:T(8,128)S(1)}, f32[1,1]{1,0:T(1,128)}) custom-call(f32[3,12,32,320]{3,2,1,0:T(8,128)} %d_hbm.1, f32[12,32,320]{2,1,0:T(8,128)} %s_hbm.1, s32[12,32,320]{2,1,0:T(8,128)} %w_hbm.1), custom_call_target="tpu_custom_call" | custom-call | flops 100000000 | bytes 4000000 | tf_op jit(solution)/shard_map/pallas_call | solution.py:595
  44.3 1.2 %copy.7 = f32[3,12,32,320]{3,2,1,0:T(8,128)} copy(f32[3,12,32,320]{3,2,1,0:T(8,128)S(1)} %get-tuple-element.6) | data formatting | bytes 2949120

commit v4 on v3

--- a/solution.py
+++ b/solution.py
@@ -20,7 +20,7 @@
 
 def kernel(
     cfg, d_hbm, s_hbm, w_hbm, out_hbm, norm_ref,
-    raw_d, raw_s, raw_w, field, last, stiff, weight, scale_b, first_out, first_in, stage, land, land_g,
+    raw_d, raw_s, raw_w, field, last, stiff, weight, scale_b, first_out, first_in, stage, land, g_out, g_in, land_g,
     rad_in, rad_g, corner, edge_s, edge_c, w_theta, w_rad, w_face, w_corner, part, gather,
     load_sem, out_sem, f_send, f_recv, t_send, t_recv, g_send, g_recv, es_send, es_recv, ec_send, ec_recv,
     rs_send, rs_recv, r0_send, r0_recv, rd_send, rd_recv, rg_send, rg_recv, c_send, c_recv, ar_send, ar_recv,
@@ -40,20 +40,23 @@
     beyond = (OFF - 1, OFF + rows)
     own = pl.ds(1, pairs)
 
-    loads = [
-        pltpu.make_async_copy(s_hbm, raw_s, load_sem.at[0]),
-        pltpu.make_async_copy(d_hbm, raw_d, load_sem.at[1]),
-        pltpu.make_async_copy(w_hbm, raw_w, load_sem.at[2]),
-    ]
-    for c in loads:
-        c.start()
-
     groups = [level(t, r) for level in levels]
     barrier = pltpu.get_barrier_semaphore()
     diagonal = [(tt, rr) for tt in beside_t for rr in beside_r]
-    greet = [(tt, r) for tt in beside_t] + diagonal + [p for g in groups for p in g]
+    greet = diagonal + [(tt, r) for tt in beside_t] + [p for g in reversed(groups) for p in g]
     for p in greet:
         pl.semaphore_signal(barrier, inc=1, device_id=p, device_id_type=MESH)
+
+    rim_loads = [
+        pltpu.make_async_copy(d_hbm.at[:, pl.ds(p, 2)], raw_d.at[:, pl.ds(p, 2)], load_sem.at[3 + side])
+        for side, p in ((0, 0), (1, 2 * pairs - 2))
+    ]
+    load_s = pltpu.make_async_copy(s_hbm, raw_s, load_sem.at[0])
+    mid = pl.ds(2, 2 * pairs - 4)
+    load_d = pltpu.make_async_copy(d_hbm.at[:, mid], raw_d.at[:, mid], load_sem.at[1])
+    load_w = pltpu.make_async_copy(w_hbm, raw_w, load_sem.at[2])
+    for c in (*rim_loads, load_s, load_d, load_w):
+        c.start()
 
     even = (iota(0) + iota(1)) % 2 == 0
     odd = jnp.logical_not(even)
@@ -87,55 +90,6 @@
     def one(row):
         return pl.ds(row, 1)
 
-    zero_row = jnp.zeros((1, LANES), F32)
-    zero = jnp.zeros((8, LANES), F32)
-    loads[0].wait()
-
-    def pack_s(k, _):
-        for i in range(tile_rows):
-            for q in range(tiles):
-                a, b = raw_tile(raw_s, (2 * k,), i, q), raw_tile(raw_s, (2 * k + 1,), i, q)
-                stiff[0, k + 1, q, at(i), :] = jnp.where(even, a, b)
-                stiff[1, k + 1, q, at(i), :] = jnp.where(even, b, a)
-        return 0
-
-    lax.fori_loop(0, pairs, pack_s, 0)
-    loads[1].wait()
-
-    def pack_d(j, _):
-        c, k = j // pairs, j % pairs
-        for i in range(tile_rows):
-            for q in range(tiles):
-                a, b = raw_tile(raw_d, (c, 2 * k), i, q), raw_tile(raw_d, (c, 2 * k + 1), i, q)
-                field[0, c, k + 1, q, at(i), :] = jnp.where(even, a, b)
-                field[1, c, k + 1, q, at(i), :] = jnp.where(even, b, a)
-        for q in range(tiles):
-            for row in beyond:
-                field[0, c, k + 1, q, one(row), :] = zero_row
-                last[c, k + 1, q, one(row), :] = zero_row
-        return 0
-
-    lax.fori_loop(0, 3 * pairs, pack_d, 0)
-    for end in range(2):
-        @pl.when(jnp.logical_not(has[end]))
-        def _():
-            def clear(k, _):
-                for q in range(tiles):
-                    stiff[0, k + 1, q, one(beyond[end]), :] = zero_row
-                    stiff[1, k + 1, q, one(beyond[end]), :] = zero_row
-                    for c in range(3):
-                        field[1, c, k + 1, q, one(beyond[end]), :] = zero_row
-                return 0
-
-            lax.fori_loop(0, pairs, clear, 0)
-
-    for c in range(3):
-        for g in ghost:
-            for q in range(tiles):
-                for i in range(tile_rows):
-                    field[0, c, g, q, at(i), :] = zero
-    loads[2].wait()
-
     def to(tt, rr):
         return {"device_id": (tt, rr), "device_id_type": MESH}
 
@@ -143,22 +97,24 @@
         return pltpu.make_async_remote_copy(src, dst, send, recv, **where)
 
     edge_copies = [
-        remote(raw_s.at[0 if side == 0 else 2 * pairs - 1], edge_s.at[1 - side], es_send.at[side], es_recv.at[1 - side], to(beside_t[side], r))
+        remote(s_hbm.at[0 if side == 0 else 2 * pairs - 1], edge_s.at[1 - side], es_send.at[side], es_recv.at[1 - side], to(beside_t[side], r))
         for side in range(2)
     ]
-    first_copies = [
-        remote(first_out.at[side], first_in.at[1 - side], f_send.at[side], f_recv.at[1 - side], to(beside_t[side], r))
-        for side in range(2)
-    ]
-
-    def theta_copies(n):
-        return [
-            remote(stage.at[n, side], land.at[n, 1 - side], t_send.at[n, side], t_recv.at[n, 1 - side], to(beside_t[side], r))
+
+    def first_copies(c):
+        return [
+            remote(first_out.at[side, c], first_in.at[1 - side, c], f_send.at[c, side], f_recv.at[c, 1 - side], to(beside_t[side], r))
             for side in range(2)
         ]
 
+    def theta_copies(n, c):
+        return [
+            remote(stage.at[n, side, c], land.at[n, 1 - side, c], t_send.at[n, c, side], t_recv.at[n, c, 1 - side], to(beside_t[side], r))
+            for side in range(2)
+        ]
+
     g_copies = [
-        remote(scale_b.at[rim[side] - 1], land_g.at[1 - side], g_send.at[side], g_recv.at[1 - side], to(beside_t[side], r))
+        remote(g_out.at[side], g_in.at[1 - side], g_send.at[side], g_recv.at[1 - side], to(beside_t[side], r))
         for side in range(2)
     ]
 
@@ -174,7 +130,7 @@
     def edge_corners(end):
         return [
             remote(
-                raw_s.at[0 if side == 0 else 2 * pairs - 1, pl.ds(0 if end == 0 else rows - 1, 1)], edge_c.at[1 - side, 1 - end],
+                s_hbm.at[0 if side == 0 else 2 * pairs - 1, pl.ds(0 if end == 0 else rows - 1, 1)], edge_c.at[1 - side, 1 - end],
                 ec_send.at[side, end], ec_recv.at[1 - side, 1 - end], to(beside_t[side], beside_r[end]),
             )
             for side in range(2)
@@ -208,11 +164,11 @@
             )
         ]
 
-    def red_corners(n, end):
+    def red_corners(n, c, end):
         return [
             remote(
-                field.at[0, slice(None), rim[side], slice(None), one(edge_row[end])], corner.at[n, 1 - side, 1 - end],
-                c_send.at[n, side, end], c_recv.at[n, 1 - side, 1 - end], to(beside_t[side], beside_r[end]),
+                field.at[0, c, rim[side], slice(None), one(edge_row[end])], corner.at[n, 1 - side, 1 - end, c],
+                c_send.at[n, c, side, end], c_recv.at[n, c, 1 - side, 1 - end], to(beside_t[side], beside_r[end]),
             )
             for side in range(2)
         ]
@@ -233,75 +189,150 @@
     low = iota(1) < half_lanes
 
     def put_folded(put, get, n):
-        for c in range(3):
-            for q in range(wide):
-                for i in range(n):
-                    put((c * wide + q) * n + i, get(c, q, i))
-        for i in range(n):
-            put(3 * wide * n + i, jnp.where(low, get(0, wide, i), pltpu.roll(get(1, wide, i), half_lanes, 1)))
+        for q in range(wide):
+            for i in range(n):
+                put(q * n + i, get(q, i))
         for i in range(n // 2):
-            x = pltpu.roll(get(2, wide, i + n // 2), half_lanes, 1)
-            put(3 * wide * n + n + i, jnp.where(low, get(2, wide, i), x))
-
-    def get_folded(load, n, c, q, i):
+            put(wide * n + i, jnp.where(low, get(wide, i), pltpu.roll(get(wide, i + n // 2), half_lanes, 1)))
+
+    def get_folded(load, n, q, i):
         if q < wide:
-            return load((c * wide + q) * n + i)
-        if c < 2:
-            x = load(3 * wide * n + i)
-            return pltpu.roll(x, half_lanes, 1) if c else x
-        x = load(3 * wide * n + n + i % (n // 2))
+            return load(q * n + i)
+        x = load(wide * n + i % (n // 2))
         return x if i < n // 2 else pltpu.roll(x, half_lanes, 1)
 
-    def send_first():
+    def pack_first(c):
         for side in range(2):
             keep = facing(1, side)
 
-            def get(c, q, h):
+            def get(q, h):
                 a = field[1, c, rim[side], q, at(2 * h), :]
                 b = field[1, c, rim[side], q, at(2 * h + 1), :]
                 return jnp.where(keep, a, pltpu.roll(b, 1, 0))
 
             def put(j, x):
-                first_out[side, pl.ds(8 * j, 8), :] = x
+                first_out[side, c, pl.ds(8 * j, 8), :] = x
 
             put_folded(put, get, tile_rows // 2)
-        for copy in first_copies:
-            copy.start()
-
-    def take_first():
-        for copy in first_copies:
+
+    def pack_g():
+        for side in range(2):
+            keep = facing(1, side)
+
+            def get(q, h):
+                a = scale_b[rim[side] - 1, q, pl.ds(16 * h, 8), :]
+                b = scale_b[rim[side] - 1, q, pl.ds(16 * h + 8, 8), :]
+                return jnp.where(keep, a, pltpu.roll(b, 1, 0))
+
+            def put(j, x):
+                g_out[side, pl.ds(8 * j, 8), :] = x
+
+            put_folded(put, get, tile_rows // 2)
+
+    def take_g():
+        for side in range(2):
+            for q in range(tiles):
+                for h in range(tile_rows // 2):
+                    x = get_folded(lambda j: g_in[side, pl.ds(8 * j, 8), :], tile_rows // 2, q, h)
+                    land_g[side, q, pl.ds(16 * h, 8), :] = x
+                    land_g[side, q, pl.ds(16 * h + 8, 8), :] = pltpu.roll(x, 7, 0)
+
+    def take_first(c):
+        for copy in first_copies(c):
             copy.wait_recv()
         for side in range(2):
-            for c in range(3):
-                for q in range(tiles):
-                    for h in range(tile_rows // 2):
-                        x = get_folded(lambda j: first_in[side, pl.ds(8 * j, 8), :], tile_rows // 2, c, q, h)
-                        field[1, c, ghost[side], q, at(2 * h), :] = x
-                        field[1, c, ghost[side], q, at(2 * h + 1), :] = pltpu.roll(x, 7, 0)
-
-    def send_theta(n):
+            for q in range(tiles):
+                for h in range(tile_rows // 2):
+                    x = get_folded(lambda j: first_in[side, c, pl.ds(8 * j, 8), :], tile_rows // 2, q, h)
+                    field[1, c, ghost[side], q, at(2 * h), :] = x
+                    field[1, c, ghost[side], q, at(2 * h + 1), :] = pltpu.roll(x, 7, 0)
+
+    def send_theta(n, c):
         for side in range(2):
             red_here = facing(0, side)
 
-            def get(c, q, i):
+            def get(q, i):
                 x = field[0, c, rim[side], q, at(i), :]
                 y = black(n)[c, rim[side], q, at(i), :]
                 return jnp.where(red_here, x, y)
 
             def put(j, x):
-                stage[n, side, pl.ds(8 * j, 8), :] = x
+                stage[n, side, c, pl.ds(8 * j, 8), :] = x
 
             put_folded(put, get, tile_rows)
-        for copy in theta_copies(n):
+        for copy in theta_copies(n, c):
             copy.start()
 
+    zero_row = jnp.zeros((1, LANES), F32)
+    zero = jnp.zeros((8, LANES), F32)
+
+    def pack_s(k, _):
+        for i in range(tile_rows):
+            for q in range(tiles):
+                a, b = raw_tile(raw_s, (2 * k,), i, q), raw_tile(raw_s, (2 * k + 1,), i, q)
+                stiff[0, k + 1, q, at(i), :] = jnp.where(even, a, b)
+                stiff[1, k + 1, q, at(i), :] = jnp.where(even, b, a)
+        return 0
+
+    def pack_d(k, _):
+        for c in range(3):
+            for i in range(tile_rows):
+                for q in range(tiles):
+                    a, b = raw_tile(raw_d, (c, 2 * k), i, q), raw_tile(raw_d, (c, 2 * k + 1), i, q)
+                    field[0, c, k + 1, q, at(i), :] = jnp.where(even, a, b)
+                    field[1, c, k + 1, q, at(i), :] = jnp.where(even, b, a)
+        return 0
+
+    def clear_rows(k, _):
+        for c in range(3):
+            for q in range(tiles):
+                for row in beyond:
+                    field[0, c, k + 1, q, one(row), :] = zero_row
+                    last[c, k + 1, q, one(row), :] = zero_row
+        return 0
+
+    for c in rim_loads:
+        c.wait()
+    lax.fori_loop(0, 2, lambda j, _: pack_d(j * (pairs - 1), 0), 0)
+    for c in range(3):
+        pack_first(c)
     pl.semaphore_wait(barrier, len(greet))
     by_end(edge_corners, "start")
-    for copy in edge_copies:
+    for copy in edge_copies + [x for c in range(3) for x in first_copies(c)]:
         copy.start()
-    send_first()
+    load_s.wait()
+    lax.fori_loop(0, pairs, pack_s, 0)
     by_end(stiff_rows, "start")
+    load_d.wait()
+    lax.fori_loop(1, pairs - 1, pack_d, 0)
     by_end(first_rows, "start")
+    lax.fori_loop(0, pairs, clear_rows, 0)
+    for end in range(2):
+        @pl.when(jnp.logical_not(has[end]))
+        def _():
+            def clear(k, _):
+                for q in range(tiles):
+                    stiff[0, k + 1, q, one(beyond[end]), :] = zero_row
+                    stiff[1, k + 1, q, one(beyond[end]), :] = zero_row
+                    for c in range(3):
+                        field[1, c, k + 1, q, one(beyond[end]), :] = zero_row
+                return 0
+
+            lax.fori_loop(0, pairs, clear, 0)
+            for side in range(2):
+                for q in range(tiles):
+                    w_corner[side, end, q] = zero_row
+                    w_face[side, end, q] = zero_row
+                    for n in range(2):
+                        for c in range(3):
+                            corner[n, side, end, c, q] = zero_row
+
+    for c in range(3):
+        for g in ghost:
+            for q in range(tiles):
+                for i in range(tile_rows):
+                    field[0, c, g, q, at(i), :] = zero
+    load_w.wait()
 
     def beside(v, side):
         out = []
@@ -356,11 +387,11 @@
                         w = jnp.where(at_first_col, 0.0, w)
                     weight[colour, f, k, q, put, :] = w
 
-    def half(colour, k, opp, cur, dst, acc=None):
+    def half(colour, k, opp, cur, dst, acc=None, comps=range(3)):
         for i in range(tile_rows):
             put = pl.ds(8 * i, 8)
             w = [[weight[colour, f, k, q, put, :] for q in range(tiles)] for f in range(7)]
-            for c in range(3):
+            for c in comps:
                 mid = [opp[c, k + 1, q, at(i), :] for q in range(tiles)]
                 forth, back = beside(mid, 1), beside(mid, 0)
                 for q in range(tiles):
@@ -381,7 +412,8 @@
         lax.fori_loop(1, pairs - 1, lambda k, _: (fn(k), 0)[1], 0)
 
     def rims(fn):
-        lax.fori_loop(0, 2, lambda j, _: (fn(j * (pairs - 1)), 0)[1], 0)
+        for k in (0, pairs - 1):
+            fn(k)
 
     def face_weights():
         for side in range(2):
@@ -434,7 +466,7 @@
 
                 lax.fori_loop(0, pairs, body, 0)
 
-    def cross_theta(n):
+    def cross_theta(n, c):
         dst = black(n)
         for side in range(2):
             k, here = rim[side], facing(1, side)
@@ -443,22 +475,17 @@
                     put = pl.ds(8 * i, 8)
                     w = jnp.where(here, weight[1, OUT, k - 1, q, put, :], 0.0)
                     wg = w_theta[side, q, put, :]
-                    for c in range(3):
-                        x = get_folded(lambda j: land[n, side, pl.ds(8 * j, 8), :], tile_rows, c, q, i)
-                        dst[c, k, q, at(i), :] = dst[c, k, q, at(i), :] + w * x
-                        dst[c, ghost[side], q, at(i), :] = x + wg * field[0, c, k, q, at(i), :]
+                    x = get_folded(lambda j: land[n, side, c, pl.ds(8 * j, 8), :], tile_rows, q, i)
+                    dst[c, k, q, at(i), :] = dst[c, k, q, at(i), :] + w * x
+                    dst[c, ghost[side], q, at(i), :] = x + wg * field[0, c, k, q, at(i), :]
         for end in range(2):
-            @pl.when(has[end])
-            def _():
-                for side in range(2):
-                    k = rim[side]
-                    for q in range(tiles):
-                        for c in range(3):
-                            x = corner[n, side, end, c, q]
-                            a = (c, ghost[side], q, one(edge_row[end]), slice(None))
-                            b = (c, k, q, one(beyond[end]), slice(None))
-                            dst[a] = dst[a] + w_corner[side, end, q] * x
-                            dst[b] = dst[b] + w_face[side, end, q] * x
+            for side in range(2):
+                for q in range(tiles):
+                    x = corner[n, side, end, c, q]
+                    a = (c, ghost[side], q, one(edge_row[end]), slice(None))
+                    b = (c, rim[side], q, one(beyond[end]), slice(None))
+                    dst[a] = dst[a] + w_corner[side, end, q] * x
+                    dst[b] = dst[b] + w_face[side, end, q] * x
 
     red, black0 = field.at[0], field.at[1]
 
@@ -475,15 +502,17 @@
                 stiff[0, ghost[side], q, at(i), :] = x
                 stiff[1, ghost[side], q, at(i), :] = x
     rims(lambda k: (make_weights(0, k), make_weights(1, k)))
+    pack_g()
     for copy in g_copies:
         copy.start()
     by_end(scale_rows, "start")
-    take_first()
-    rims(lambda k: half(0, k, black0, red, red))
-    by_end(functools.partial(red_corners, 0), "start")
     by_end(first_rows, "drain")
-    rims(lambda k: half(1, k, red, black0, black0))
-    send_theta(0)
+    for c in range(3):
+        take_first(c)
+        rims(lambda k: half(0, k, black0, red, red, comps=(c,)))
+        by_end(functools.partial(red_corners, 0, c), "start")
+        rims(lambda k: half(1, k, red, black0, black0, comps=(c,)))
+        send_theta(0, c)
     inner(lambda k: half(1, k, red, black0, black0))
     by_end(functools.partial(both_rows, 0), "start")
 
@@ -492,27 +521,30 @@
     by_end(functools.partial(both_rows, 0), "take")
     by_end(functools.partial(both_rows, 0), "drain")
     cross_rad(0)
-    by_end(functools.partial(red_corners, 0), "drain")
+    for c in range(3):
+        by_end(functools.partial(red_corners, 0, c), "drain")
     inner(lambda k: half(0, k, black0, red, red))
     for copy in g_copies:
         copy.wait_recv()
+    take_g()
     by_end(edge_corners, "take")
     face_weights()
-    for copy in theta_copies(0):
-        copy.wait_recv()
-    by_end(functools.partial(red_corners, 0), "take")
-    cross_theta(0)
-    rims(lambda k: half(0, k, black0, red, red))
-    by_end(functools.partial(red_corners, 1), "start")
-    rims(lambda k: half(1, k, red, black0, last))
-    send_theta(1)
+    for c in range(3):
+        for copy in theta_copies(0, c):
+            copy.wait_recv()
+        by_end(functools.partial(red_corners, 0, c), "take")
+        cross_theta(0, c)
+        rims(lambda k: half(0, k, black0, red, red, comps=(c,)))
+        by_end(functools.partial(red_corners, 1, c), "start")
+        rims(lambda k: half(1, k, red, black0, last, comps=(c,)))
+        send_theta(1, c)
     inner(lambda k: half(1, k, red, black0, last))
     by_end(functools.partial(both_rows, 1), "start")
 
-    def squares(k, acc):
+    def squares(k, acc, comps=range(3)):
         for i in range(tile_rows):
             for q in range(tiles):
-                for c in range(3):
+                for c in comps:
                     change = last[c, k + 1, q, at(i), :] - field[1, c, k + 1, q, at(i), :]
                     acc = acc + change * change
         return acc
@@ -522,12 +554,14 @@
     cross_rad(1)
     red_sum = lax.fori_loop(1, pairs - 1, lambda k, a: half(0, k, last, red, None, a), zero)
     black_sum = lax.fori_loop(1, pairs - 1, squares, zero)
-    for copy in theta_copies(1):
-        copy.wait_recv()
-    by_end(functools.partial(red_corners, 1), "take")
-    cross_theta(1)
-    red_sum = lax.fori_loop(0, 2, lambda j, a: half(0, j * (pairs - 1), last, red, None, a), red_sum)
-    black_sum = lax.fori_loop(0, 2, lambda j, a: squares(j * (pairs - 1), a), black_sum)
+    for c in range(3):
+        for copy in theta_copies(1, c):
+            copy.wait_recv()
+        by_end(functools.partial(red_corners, 1, c), "take")
+        cross_theta(1, c)
+        for k in (0, pairs - 1):
+            red_sum = half(0, k, last, red, None, red_sum, comps=(c,))
+            black_sum = squares(k, black_sum, comps=(c,))
 
     part[0] = jnp.sum(black_sum * (1.0 / 9.0) + red_sum * (1.0 / 2.25), axis=0, keepdims=True)
     for level, peers in enumerate(groups):
@@ -557,9 +591,9 @@
     for level, peers in enumerate(groups):
         everything = gather.at[level, pl.ds(0, len(peers))]
         pltpu.make_async_copy(everything, everything, ar_send.at[level]).wait()
-    for copy in edge_copies + first_copies + g_copies + theta_copies(0) + theta_copies(1):
+    for copy in edge_copies + g_copies + [x for c in range(3) for x in first_copies(c) + theta_copies(0, c) + theta_copies(1, c)]:
         copy.wait_send()
-    for copies in (stiff_rows, edge_corners, scale_rows, functools.partial(red_corners, 1)):
+    for copies in (stiff_rows, edge_corners, scale_rows, *(functools.partial(red_corners, 1, c) for c in range(3))):
         by_end(copies, "drain")
     pltpu.make_async_copy(raw_d, out_hbm, out_sem.at[0]).wait()
 
@@ -588,7 +622,7 @@
     def shards(displacement, stiffness, wall):
         planes, rows, cols = stiffness.shape
         pairs, tiles = planes // 2, -(-cols // LANES)
-        folded = 3 * (tiles - 1) * rows + rows + rows // 2
+        folded = (tiles - 1) * rows + rows // 2
         count = 3.0 * planes * rows * cols * n_theta * n_rad
         cfg = (n_theta, n_rad, pairs, rows, cols, tiles, levels, count)
         dma = pltpu.SemaphoreType.DMA
@@ -606,10 +640,12 @@
                 pltpu.VMEM((2, pairs + 2, tiles, rows + 16, LANES), F32),
                 pltpu.VMEM((2, 7, pairs, tiles, rows, LANES), F32),
                 pltpu.VMEM((pairs, tiles, rows, LANES), F32),
+                pltpu.VMEM((2, 3, folded // 2, LANES), F32),
+                pltpu.VMEM((2, 3, folded // 2, LANES), F32),
+                pltpu.VMEM((2, 2, 3, folded, LANES), F32),
+                pltpu.VMEM((2, 2, 3, folded, LANES), F32),
                 pltpu.VMEM((2, folded // 2, LANES), F32),
                 pltpu.VMEM((2, folded // 2, LANES), F32),
-                pltpu.VMEM((2, 2, folded, LANES), F32),
-                pltpu.VMEM((2, 2, folded, LANES), F32),
                 pltpu.VMEM((2, tiles, rows, LANES), F32),
                 pltpu.VMEM((2, 2, 2, 3, pairs, tiles, 1, LANES), F32),
                 pltpu.VMEM((2, pairs, tiles, 1, LANES), F32),
@@ -622,9 +658,9 @@
                 pltpu.VMEM((2, 2, tiles, 1, LANES), F32),
                 pltpu.VMEM((3, 1, LANES), F32),
                 pltpu.VMEM((2, -(-max(sizes) // 8) * 8, LANES), F32),
-                dma((3,)), dma((1,)), dma((2,)), dma((2,)), dma((2, 2)), dma((2, 2)), dma((2,)), dma((2,)),
+                dma((5,)), dma((1,)), dma((3, 2)), dma((3, 2)), dma((2, 3, 2)), dma((2, 3, 2)), dma((2,)), dma((2,)),
                 dma((2,)), dma((2,)), dma((2, 2)), dma((2, 2)), dma((2, 2)), dma((2, 2)), dma((2,)), dma((2,)),
-                dma((2, 2, 2)), dma((2, 2, 2)), dma((2,)), dma((2,)), dma((2, 2, 2)), dma((2, 2, 2)), dma((2,)), dma((2,)),
+                dma((2, 2, 2)), dma((2, 2, 2)), dma((2,)), dma((2,)), dma((2, 3, 2, 2)), dma((2, 3, 2, 2)), dma((2,)), dma((2,)),
             ],
             compiler_params=pltpu.CompilerParams(collective_id=0, has_side_effects=True, vmem_limit_bytes=56 * 2**20),
             cost_estimate=pl.CostEstimate(flops=10**8, bytes_accessed=4 * 10**6, transcendentals=0),

time: 47.3 us -> 45 us (0.951)
  Pallas kernels: 43.6 us -> 41.3 us
    pallas_call x1, Pallas kernels: 43.6 us -> 41.3 us  [shards(): pl.pallas_call(functools.partial(kernel, cfg), out_shape=(pltpu.VMEM(disp...]
where the time goes in v4:
time: 45 us; the launch traced here: 44.9 us
  Pallas kernels  41.3 us (92%)
  between operations  2.33 us (5%)
  local copies, waits for them, and re-layouts  1.21 us (3%)
    pallas_call x1, Pallas kernels, shards(): pl.pallas_call(functools.partial(kernel, cfg), out_shape=(pltpu.VMEM(disp...  41.3 us
    unnamed x1, local copies, waits for them, and re-layouts  1.21 us

profile of v4, /device:TPU:1, one launch (start us, length us, event | category | flops | bytes accessed | tf_op | source)
XLA Modules:
  0.0 44.9 jit_solution(950991351452852437)
XLA Ops:
  0.6 41.3 %shard_map.50 = (f32[3,12,32,320]{3,2,1,0:T(8,128)S(1)}, f32[1,1]{1,0:T(1,128)}) custom-call(f32[3,12,32,320]{3,2,1,0:T(8,128)} %d_hbm.1, f32[12,32,320]{2,1,0:T(8,128)} %s_hbm.1, s32[12,32,320]{2,1,0:T(8,128)} %w_hbm.1), custom_call_target="tpu_custom_call" | custom-call | flops 100000000 | bytes 4000000 | tf_op jit(solution)/shard_map/pallas_call | solution.py:629
  42.0 1.2 %copy.7 = f32[3,12,32,320]{3,2,1,0:T(8,128)} copy(f32[3,12,32,320]{3,2,1,0:T(8,128)S(1)} %get-tuple-element.6) | data formatting | bytes 2949120

commit v5 on v4

--- a/solution.py
+++ b/solution.py
@@ -445,7 +445,8 @@
                         w_rad[end, k, q] = (stiff[1, k + 1, q, one(beyond[end]), :] + stiff[0, k + 1, q, one(edge_row[end]), :]) * rad_g[end, k, q]
                     return 0
 
-                lax.fori_loop(0, pairs, body, 0)
+                for k in range(pairs):
+                    body(k, 0)
 
     def cross_rad(n):
         dst = black(n)
@@ -464,7 +465,8 @@
                             dst[c, k + 1, q, one(beyond[end]), :] = rad_in[n, 1, end, c, k, q] + wg * field[(0, *here)]
                     return 0
 
-                lax.fori_loop(0, pairs, body, 0)
+                for k in range(pairs):
+                    body(k, 0)
 
     def cross_theta(n, c):
         dst = black(n)

time: 45 us -> 45 us (level)
  no operation moved by 1% of the time
where the time goes in v5:
time: 45 us; the launch traced here: 44.9 us
  Pallas kernels  41.3 us (92%)
  between operations  2.33 us (5%)
  local copies, waits for them, and re-layouts  1.21 us (3%)
    pallas_call x1, Pallas kernels, shards(): pl.pallas_call(functools.partial(kernel, cfg), out_shape=(pltpu.VMEM(disp...  41.3 us
    unnamed x1, local copies, waits for them, and re-layouts  1.21 us

profile of v5, /device:TPU:1, one launch (start us, length us, event | category | flops | bytes accessed | tf_op | source)
XLA Modules:
  0.0 44.9 jit_solution(2753202706820547144)
XLA Ops:
  0.6 41.3 %shard_map.50 = (f32[3,12,32,320]{3,2,1,0:T(8,128)S(1)}, f32[1,1]{1,0:T(1,128)}) custom-call(f32[3,12,32,320]{3,2,1,0:T(8,128)} %d_hbm.1, f32[12,32,320]{2,1,0:T(8,128)} %s_hbm.1, s32[12,32,320]{2,1,0:T(8,128)} %w_hbm.1), custom_call_target="tpu_custom_call" | custom-call | flops 100000000 | bytes 4000000 | tf_op jit(solution)/shard_map/pallas_call | solution.py:631
  42.0 1.2 %copy.7 = f32[3,12,32,320]{3,2,1,0:T(8,128)} copy(f32[3,12,32,320]{3,2,1,0:T(8,128)S(1)} %get-tuple-element.6) | data formatting | bytes 2949120
